TPU v7x, 512 devices: a whole 4x8x8 slice. The times are simulated.
512 devices in a mesh: seq: 512 (over x, z, y, core).
Axes of the slice: x: 4, y: 8, z: 8, core: 2. Of those that a mesh axis runs over, the one named last changes fastest.
Arguments:
- queries: bfloat16 [196608, 1024], P('seq')
- keys: bfloat16 [196608, 256], P('seq')
- values: bfloat16 [196608, 256], P('seq'), may hold values from -6 to 6
- out_weight: bfloat16 [1024, 2048], replicated, may hold values from -9 to 9
Outputs:
- projected: bfloat16 [196608, 2048], P('seq')
All inputs are finite; a program needn't handle non-finite values.
Results may differ from a plain program's by a relative error of at most 0.0057.
Values may be sent and summed in bfloat16 or wider, within the bound.
No kernel may reach another device: no remote copies, remote signals or barrier semaphores. Data moves between devices by JAX's collectives and lax.ppermute only.
A program may use at most 64 MiB of HBM per device.

v0:
```python
import jax
import jax.numpy as jnp
from jax import lax
from jax.sharding import PartitionSpec as P


def from_behind(block, axis, distance):
    devices = range(lax.axis_size(axis))
    route = [(i - distance, i) for i in devices if i - distance in devices]
    return lax.ppermute(block, axis, route)


def on_device(queries, keys, values, out_weight):
    tok_rows = queries.shape[0]
    reach = tok_rows // 2
    head_size = 128
    heads = queries.shape[1] // head_size
    kv_heads = keys.shape[1] // head_size
    group = heads // kv_heads
    scale = 1.0 / head_size**0.5
    where_am = lax.axis_index("seq")
    earlier_keys, earlier_values = from_behind(
        (keys[tok_rows - reach :], values[tok_rows - reach :]), "seq", 1
    )
    key_parts = [earlier_keys, keys]
    value_parts = [earlier_values, values]
    for distance in (2, 4, 8, 16):
        far_keys, far_values = from_behind((keys, values), "seq", distance)
        key_parts.append(far_keys)
        value_parts.append(far_values)
    span = reach + 5 * tok_rows
    rows = jnp.arange(tok_rows, dtype=jnp.int32)[:, None]
    offset = jnp.arange(reach + tok_rows, dtype=jnp.int32)[None, :] - reach
    near = (offset <= rows) & (offset >= rows - reach) & ((offset >= 0) | (where_am >= 1))
    mask_parts = [near]
    for distance in (2, 4, 8, 16):
        mask_parts.append(jnp.broadcast_to(where_am >= distance, (tok_rows, tok_rows)))
    allowed = jnp.concatenate(mask_parts, axis=1)
    key_heads = jnp.transpose(
        jnp.concatenate(key_parts, axis=0).reshape(span, kv_heads, head_size), (1, 0, 2)
    )
    value_heads = jnp.transpose(
        jnp.concatenate(value_parts, axis=0).reshape(span, kv_heads, head_size), (1, 0, 2)
    )
    query_heads = jnp.transpose(queries.reshape(tok_rows, heads, head_size), (1, 0, 2))

    def one_head(head):
        query_one = query_heads[head]
        key_one = key_heads[head // group]
        value_one = value_heads[head // group]
        scores = (
            lax.dot_general(
                query_one, key_one, (((1,), (1,)), ((), ())), preferred_element_type=jnp.float32
            )
            * scale
        )
        scores = jnp.where(allowed, scores, -1e30)
        top = jnp.max(scores, axis=-1, keepdims=True)
        weights = jnp.where(allowed, jnp.exp(scores - top), 0.0)
        totals = jnp.sum(weights, axis=-1, keepdims=True)
        summed = jnp.dot(
            weights.astype(jnp.bfloat16), value_one, preferred_element_type=jnp.float32
        )
        return (summed / totals).astype(jnp.bfloat16)

    attended = lax.map(one_head, jnp.arange(heads, dtype=jnp.int32))
    attended = jnp.transpose(attended, (1, 0, 2)).reshape(tok_rows, heads * head_size)
    projected = jnp.dot(attended, out_weight, preferred_element_type=jnp.float32)
    return projected.astype(jnp.bfloat16)


def solution(mesh):
    in_specs = (P("seq", None), P("seq", None), P("seq", None), P())
    out_specs = P("seq", None)
    return jax.shard_map(
        on_device, mesh=mesh, in_specs=in_specs, out_specs=out_specs, check_vma=False
    )
```

profile of v0, /device:TPU:6, one launch (start us, length us, event | category | flops | bytes accessed | tf_op | source)
XLA Modules:
  0.0 157.3 jit_solution(212289953345751422)
XLA Ops:
  0.0 3.5 %collective-permute-start.6 = (bf16[384,256]{1,0:T(8,128)(2,1)}, bf16[384,256]{1,0:T(8,128)(2,1)S(1)}, u32[]{:S(2)}, u32[]{:S(2)}) collective-permute-start(bf16[384,256]{1,0:T(8,128)(2,1)} %param.8), channel_id=1, source_target_pairs={{0,2},{1,3},{2,4},{3,5},{4,6},{5,7},{6,8},{7,9},{8,10},{9,11},{10,... | collective-permute-start | bytes 589832 | tf_op jit(solution)/shard_map/ppermute | solution.py:10
  3.5 4.5 %collective-permute-start.7 = (bf16[384,256]{1,0:T(8,128)(2,1)}, bf16[384,256]{1,0:T(8,128)(2,1)S(1)}, u32[]{:S(2)}, u32[]{:S(2)}) collective-permute-start(bf16[384,256]{1,0:T(8,128)(2,1)} %param.8), channel_id=1, source_target_pairs={{0,4},{1,5},{2,6},{3,7},{4,8},{5,9},{6,10},{7,11},{8,12},{9,13},{1... | collective-permute-start | bytes 589832 | tf_op jit(solution)/shard_map/ppermute | solution.py:10
  8.0 5.0 %collective-permute-start.8 = (bf16[384,256]{1,0:T(8,128)(2,1)}, bf16[384,256]{1,0:T(8,128)(2,1)S(1)}, u32[]{:S(2)}, u32[]{:S(2)}) collective-permute-start(bf16[384,256]{1,0:T(8,128)(2,1)} %param.8), channel_id=1, source_target_pairs={{0,8},{1,9},{2,10},{3,11},{4,12},{5,13},{6,14},{7,15},{8,16},{9,17... | collective-permute-start | bytes 589832 | tf_op jit(solution)/shard_map/ppermute | solution.py:10
  13.0 4.3 %collective-permute-start.9 = (bf16[384,256]{1,0:T(8,128)(2,1)}, bf16[384,256]{1,0:T(8,128)(2,1)S(1)}, u32[]{:S(2)}, u32[]{:S(2)}) collective-permute-start(bf16[384,256]{1,0:T(8,128)(2,1)} %param.8), channel_id=1, source_target_pairs={{0,16},{1,17},{2,18},{3,19},{4,20},{5,21},{6,22},{7,23},{8,24},{9,... | collective-permute-start | bytes 589832 | tf_op jit(solution)/shard_map/ppermute | solution.py:10
  17.3 0.9 slice.7
  18.2 1.9 %collective-permute-start.5 = (bf16[192,256]{1,0:T(8,128)(2,1)S(1)}, bf16[192,256]{1,0:T(8,128)(2,1)S(1)}, u32[]{:S(2)}, u32[]{:S(2)}) collective-permute-start(bf16[192,256]{1,0:T(8,128)(2,1)S(1)} %slice.7), channel_id=1, source_target_pairs={{0,1},{1,2},{2,3},{3,4},{4,5},{5,6},{6,7},{7,8},{8,9},{9,10},{10,1... | collective-permute-start | bytes 294920 | tf_op jit(solution)/shard_map/ppermute | solution.py:10
  21.8 1.2 copy.5
  23.0 13.0 %collective-permute-done.5 = bf16[192,256]{1,0:T(8,128)(2,1)S(1)} collective-permute-done((bf16[192,256]{1,0:T(8,128)(2,1)S(1)}, bf16[192,256]{1,0:T(8,128)(2,1)S(1)}, u32[]{:S(2)}, u32[]{:S(2)}) %collective-permute-start.5) | collective-permute-done | bytes 98336 | tf_op jit(solution)/shard_map/ppermute | solution.py:10
  36.0 1.9 %collective-permute-start = (bf16[192,256]{1,0:T(8,128)(2,1)S(1)}, bf16[192,256]{1,0:T(8,128)(2,1)S(1)}, u32[]{:S(2)}, u32[]{:S(2)}) collective-permute-start(bf16[192,256]{1,0:T(8,128)(2,1)S(1)} %slice.6), channel_id=1, source_target_pairs={{0,1},{1,2},{2,3},{3,4},{4,5},{5,6},{6,7},{7,8},{8,9},{9,10},{10,1... | collective-permute-start | bytes 294920 | tf_op jit(solution)/shard_map/ppermute | solution.py:10
  38.0 8.2 %collective-permute-done = bf16[192,256]{1,0:T(8,128)(2,1)S(1)} collective-permute-done((bf16[192,256]{1,0:T(8,128)(2,1)S(1)}, bf16[192,256]{1,0:T(8,128)(2,1)S(1)}, u32[]{:S(2)}, u32[]{:S(2)}) %collective-permute-start) | collective-permute-done | bytes 98336 | tf_op jit(solution)/shard_map/ppermute | solution.py:10
  46.1 1.9 %collective-permute-start.1 = (bf16[384,256]{1,0:T(8,128)(2,1)S(1)}, bf16[384,256]{1,0:T(8,128)(2,1)S(1)}, u32[]{:S(2)}, u32[]{:S(2)}) collective-permute-start(bf16[384,256]{1,0:T(8,128)(2,1)S(1)} %copy-done.3), channel_id=1, source_target_pairs={{0,2},{1,3},{2,4},{3,5},{4,6},{5,7},{6,8},{7,9},{8,10},{9,11},{10,... | collective-permute-start | bytes 589832 | tf_op jit(solution)/shard_map/ppermute | solution.py:10
  49.4 1.9 %collective-permute-start.2 = (bf16[384,256]{1,0:T(8,128)(2,1)S(1)}, bf16[384,256]{1,0:T(8,128)(2,1)}, u32[]{:S(2)}, u32[]{:S(2)}) collective-permute-start(bf16[384,256]{1,0:T(8,128)(2,1)S(1)} %copy-done.3), channel_id=1, source_target_pairs={{0,4},{1,5},{2,6},{3,7},{4,8},{5,9},{6,10},{7,11},{8,12},{9,13},{1... | collective-permute-start | bytes 589832 | tf_op jit(solution)/shard_map/ppermute | solution.py:10
  51.4 1.9 %collective-permute-start.3 = (bf16[384,256]{1,0:T(8,128)(2,1)S(1)}, bf16[384,256]{1,0:T(8,128)(2,1)}, u32[]{:S(2)}, u32[]{:S(2)}) collective-permute-start(bf16[384,256]{1,0:T(8,128)(2,1)S(1)} %copy-done.3), channel_id=1, source_target_pairs={{0,8},{1,9},{2,10},{3,11},{4,12},{5,13},{6,14},{7,15},{8,16},{9,17... | collective-permute-start | bytes 589832 | tf_op jit(solution)/shard_map/ppermute | solution.py:10
  53.3 1.9 %collective-permute-start.4 = (bf16[384,256]{1,0:T(8,128)(2,1)S(1)}, bf16[384,256]{1,0:T(8,128)(2,1)}, u32[]{:S(2)}, u32[]{:S(2)}) collective-permute-start(bf16[384,256]{1,0:T(8,128)(2,1)S(1)} %copy-done.3), channel_id=1, source_target_pairs={{0,16},{1,17},{2,18},{3,19},{4,20},{5,21},{6,22},{7,23},{8,24},{9,... | collective-permute-start | bytes 589832 | tf_op jit(solution)/shard_map/ppermute | solution.py:10
  55.3 0.8 copy.7
  56.1 1.4 copy.10
  57.5 12.8 %collective-permute-done.1 = bf16[384,256]{1,0:T(8,128)(2,1)S(1)} collective-permute-done((bf16[384,256]{1,0:T(8,128)(2,1)S(1)}, bf16[384,256]{1,0:T(8,128)(2,1)S(1)}, u32[]{:S(2)}, u32[]{:S(2)}) %collective-permute-start.1) | collective-permute-done | bytes 196640 | tf_op jit(solution)/shard_map/ppermute | solution.py:10
  71.0 1.6 %constant_dynamic-update-slice_fusion.3 = bf16[2112,256]{1,0:T(8,128)(2,1)} fusion(bf16[2112,256]{1,0:T(8,128)(2,1)} %constant_dynamic-update-slice_fusion.4, bf16[384,256]{1,0:T(8,128)(2,1)} %collective-permute-done.2), kind=kLoop, calls=%fused_computation.32 | loop fusion | bytes 393216
  72.6 1.6 %constant_dynamic-update-slice_fusion.2 = bf16[2112,256]{1,0:T(8,128)(2,1)} fusion(bf16[2112,256]{1,0:T(8,128)(2,1)} %constant_dynamic-update-slice_fusion.3, bf16[384,256]{1,0:T(8,128)(2,1)} %collective-permute-done.3), kind=kLoop, calls=%fused_computation.31 | loop fusion | bytes 393216
  74.3 1.6 %constant_dynamic-update-slice_fusion.1 = bf16[2112,256]{1,0:T(8,128)(2,1)} fusion(bf16[2112,256]{1,0:T(8,128)(2,1)} %constant_dynamic-update-slice_fusion.2, bf16[384,256]{1,0:T(8,128)(2,1)} %collective-permute-done.4), kind=kLoop, calls=%fused_computation.30 | loop fusion | bytes 393216 | tf_op jit(solution)/shard_map/concatenate | solution.py:40
  75.9 1.6 %copy.6 = bf16[2112,256]{0,1:T(8,128)(2,1)S(1)} copy(bf16[2112,256]{1,0:T(8,128)(2,1)} %constant_dynamic-update-slice_fusion.1) | data formatting | bytes 2162688 | tf_op jit(solution)/shard_map/concatenate | solution.py:40
  77.5 0.7 copy.9
  78.3 73.6 %while.12 = (s32[]{:T(128)}, bf16[8,384,128]{1,2,0:T(8,128)(2,1)}, s32[8]{0:T(128)S(1)}, bf16[8,384,128]{1,2,0:T(8,128)(2,1)}, bf16[2,2112,128]{2,1,0:T(8,128)(2...) while((s32[]{:T(128)}, bf16[8,384,128]{1,2,0:T(8,128)(2,1)}, ...), condition=%wide.region_3.4_spmd, body=%wide.region_0.3_spmd.sunk | while | flops 422632704 | bytes 18171264 | solution.py:66
  82.8 1.6 %fusion.38 = (f32[384]{0:T(512)S(1)}, f32[384,2112]{0,1:T(8,128)S(1)}) fusion(pred[384,2112]{0,1:T(32,128)(4,1)S(1)} %get-tuple-element.197, bf16[8,384,128]{1,2,0:T(8,128)(2,1)} %get-tuple-element.195, s32[]{:T(128)S(6)} %select_n.55, bf16[2,2112,128]{2,1,0:T(8,128)(2,1)S(1)} %get-tuple-element.196, s32[]{:T(128)S(6)} %select_n.57), kind=kOutput, calls=%fused_computation.45.clone.1 | convolution fusion | flops 210050688 | bytes 4695560 | tf_op jit(solution)/shard_map/while/body/eval_jaxpr/dot_general | solution.py:52
  84.4 0.9 fusion.39
  85.6 1.1 fusion.40
  92.0 1.6 %fusion.38 = (f32[384]{0:T(512)S(1)}, f32[384,2112]{0,1:T(8,128)S(1)}) fusion(pred[384,2112]{0,1:T(32,128)(4,1)S(1)} %get-tuple-element.197, bf16[8,384,128]{1,2,0:T(8,128)(2,1)} %get-tuple-element.195, s32[]{:T(128)S(6)} %select_n.55, bf16[2,2112,128]{2,1,0:T(8,128)(2,1)S(1)} %get-tuple-element.196, s32[]{:T(128)S(6)} %select_n.57), kind=kOutput, calls=%fused_computation.45.clone.1 | convolution fusion | flops 210050688 | bytes 4695560 | tf_op jit(solution)/shard_map/while/body/eval_jaxpr/dot_general | solution.py:52
  93.6 0.9 fusion.39
  94.8 1.1 fusion.40
  101.2 1.6 %fusion.38 = (f32[384]{0:T(512)S(1)}, f32[384,2112]{0,1:T(8,128)S(1)}) fusion(pred[384,2112]{0,1:T(32,128)(4,1)S(1)} %get-tuple-element.197, bf16[8,384,128]{1,2,0:T(8,128)(2,1)} %get-tuple-element.195, s32[]{:T(128)S(6)} %select_n.55, bf16[2,2112,128]{2,1,0:T(8,128)(2,1)S(1)} %get-tuple-element.196, s32[]{:T(128)S(6)} %select_n.57), kind=kOutput, calls=%fused_computation.45.clone.1 | convolution fusion | flops 210050688 | bytes 4695560 | tf_op jit(solution)/shard_map/while/body/eval_jaxpr/dot_general | solution.py:52
  102.8 0.9 fusion.39
  104.0 1.1 fusion.40
  110.4 1.6 %fusion.38 = (f32[384]{0:T(512)S(1)}, f32[384,2112]{0,1:T(8,128)S(1)}) fusion(pred[384,2112]{0,1:T(32,128)(4,1)S(1)} %get-tuple-element.197, bf16[8,384,128]{1,2,0:T(8,128)(2,1)} %get-tuple-element.195, s32[]{:T(128)S(6)} %select_n.55, bf16[2,2112,128]{2,1,0:T(8,128)(2,1)S(1)} %get-tuple-element.196, s32[]{:T(128)S(6)} %select_n.57), kind=kOutput, calls=%fused_computation.45.clone.1 | convolution fusion | flops 210050688 | bytes 4695560 | tf_op jit(solution)/shard_map/while/body/eval_jaxpr/dot_general | solution.py:52
  112.0 0.9 fusion.39
  113.2 1.1 fusion.40
  119.6 1.6 %fusion.38 = (f32[384]{0:T(512)S(1)}, f32[384,2112]{0,1:T(8,128)S(1)}) fusion(pred[384,2112]{0,1:T(32,128)(4,1)S(1)} %get-tuple-element.197, bf16[8,384,128]{1,2,0:T(8,128)(2,1)} %get-tuple-element.195, s32[]{:T(128)S(6)} %select_n.55, bf16[2,2112,128]{2,1,0:T(8,128)(2,1)S(1)} %get-tuple-element.196, s32[]{:T(128)S(6)} %select_n.57), kind=kOutput, calls=%fused_computation.45.clone.1 | convolution fusion | flops 210050688 | bytes 4695560 | tf_op jit(solution)/shard_map/while/body/eval_jaxpr/dot_general | solution.py:52
  121.2 0.9 fusion.39
  122.4 1.1 fusion.40
  128.8 1.6 %fusion.38 = (f32[384]{0:T(512)S(1)}, f32[384,2112]{0,1:T(8,128)S(1)}) fusion(pred[384,2112]{0,1:T(32,128)(4,1)S(1)} %get-tuple-element.197, bf16[8,384,128]{1,2,0:T(8,128)(2,1)} %get-tuple-element.195, s32[]{:T(128)S(6)} %select_n.55, bf16[2,2112,128]{2,1,0:T(8,128)(2,1)S(1)} %get-tuple-element.196, s32[]{:T(128)S(6)} %select_n.57), kind=kOutput, calls=%fused_computation.45.clone.1 | convolution fusion | flops 210050688 | bytes 4695560 | tf_op jit(solution)/shard_map/while/body/eval_jaxpr/dot_general | solution.py:52
  130.4 0.9 fusion.39
  131.6 1.1 fusion.40
  138.0 1.6 %fusion.38 = (f32[384]{0:T(512)S(1)}, f32[384,2112]{0,1:T(8,128)S(1)}) fusion(pred[384,2112]{0,1:T(32,128)(4,1)S(1)} %get-tuple-element.197, bf16[8,384,128]{1,2,0:T(8,128)(2,1)} %get-tuple-element.195, s32[]{:T(128)S(6)} %select_n.55, bf16[2,2112,128]{2,1,0:T(8,128)(2,1)S(1)} %get-tuple-element.196, s32[]{:T(128)S(6)} %select_n.57), kind=kOutput, calls=%fused_computation.45.clone.1 | convolution fusion | flops 210050688 | bytes 4695560 | tf_op jit(solution)/shard_map/while/body/eval_jaxpr/dot_general | solution.py:52
  139.6 0.9 fusion.39
  140.8 1.1 fusion.40
  147.2 1.6 %fusion.38 = (f32[384]{0:T(512)S(1)}, f32[384,2112]{0,1:T(8,128)S(1)}) fusion(pred[384,2112]{0,1:T(32,128)(4,1)S(1)} %get-tuple-element.197, bf16[8,384,128]{1,2,0:T(8,128)(2,1)} %get-tuple-element.195, s32[]{:T(128)S(6)} %select_n.55, bf16[2,2112,128]{2,1,0:T(8,128)(2,1)S(1)} %get-tuple-element.196, s32[]{:T(128)S(6)} %select_n.57), kind=kOutput, calls=%fused_computation.45.clone.1 | convolution fusion | flops 210050688 | bytes 4695560 | tf_op jit(solution)/shard_map/while/body/eval_jaxpr/dot_general | solution.py:52
  148.8 0.9 fusion.39
  150.0 1.1 fusion.40
  151.9 5.4 %convolution_convert_fusion = bf16[384,2048]{1,0:T(8,128)(2,1)} fusion(bf16[384,1024]{0,1:T(8,128)(2,1)} %bitcast.44, bf16[1024,2048]{1,0:T(8,128)(2,1)} %param.9), kind=kOutput, calls=%fused_computation.21 | convolution fusion | flops 1611399168 | bytes 6553600 | tf_op jit(solution)/shard_map/dot_general | solution.py:68
  (74 shorter events, 17.4 us)
Async XLA Ops:
  0.0 49.4 %collective-permute-start.6 = (bf16[384,256]{1,0:T(8,128)(2,1)}, bf16[384,256]{1,0:T(8,128)(2,1)S(1)}, u32[]{:S(2)}, u32[]{:S(2)}) collective-permute-start(bf16[384,256]{1,0:T(8,128)(2,1)} %param.8), channel_id=1, source_target_pairs={{0,2},{1,3},{2,4},{3,5},{4,6},{5,7},{6,8},{7,9},{8,10},{9,11},{10,... | collective-permute-start | bytes 589832 | tf_op jit(solution)/shard_map/ppermute | solution.py:10
  3.5 47.9 %collective-permute-start.7 = (bf16[384,256]{1,0:T(8,128)(2,1)}, bf16[384,256]{1,0:T(8,128)(2,1)S(1)}, u32[]{:S(2)}, u32[]{:S(2)}) collective-permute-start(bf16[384,256]{1,0:T(8,128)(2,1)} %param.8), channel_id=1, source_target_pairs={{0,4},{1,5},{2,6},{3,7},{4,8},{5,9},{6,10},{7,11},{8,12},{9,13},{1... | collective-permute-start | bytes 589832 | tf_op jit(solution)/shard_map/ppermute | solution.py:10
  8.0 45.3 %collective-permute-start.8 = (bf16[384,256]{1,0:T(8,128)(2,1)}, bf16[384,256]{1,0:T(8,128)(2,1)S(1)}, u32[]{:S(2)}, u32[]{:S(2)}) collective-permute-start(bf16[384,256]{1,0:T(8,128)(2,1)} %param.8), channel_id=1, source_target_pairs={{0,8},{1,9},{2,10},{3,11},{4,12},{5,13},{6,14},{7,15},{8,16},{9,17... | collective-permute-start | bytes 589832 | tf_op jit(solution)/shard_map/ppermute | solution.py:10
  13.0 42.2 %collective-permute-start.9 = (bf16[384,256]{1,0:T(8,128)(2,1)}, bf16[384,256]{1,0:T(8,128)(2,1)S(1)}, u32[]{:S(2)}, u32[]{:S(2)}) collective-permute-start(bf16[384,256]{1,0:T(8,128)(2,1)} %param.8), channel_id=1, source_target_pairs={{0,16},{1,17},{2,18},{3,19},{4,20},{5,21},{6,22},{7,23},{8,24},{9,... | collective-permute-start | bytes 589832 | tf_op jit(solution)/shard_map/ppermute | solution.py:10
  18.2 17.8 %collective-permute-start.5 = (bf16[192,256]{1,0:T(8,128)(2,1)S(1)}, bf16[192,256]{1,0:T(8,128)(2,1)S(1)}, u32[]{:S(2)}, u32[]{:S(2)}) collective-permute-start(bf16[192,256]{1,0:T(8,128)(2,1)S(1)} %slice.7), channel_id=1, source_target_pairs={{0,1},{1,2},{2,3},{3,4},{4,5},{5,6},{6,7},{7,8},{8,9},{9,10},{10,1... | collective-permute-start | bytes 294920 | tf_op jit(solution)/shard_map/ppermute | solution.py:10
  20.5 0.9 copy-start.3
  20.6 1.2 copy-start.1
  21.4 16.5 %copy-start.2 = (bf16[384,256]{1,0:T(8,128)(2,1)S(1)}, bf16[384,256]{1,0:T(8,128)(2,1)}, u32[]{:S(2)}) copy-start(bf16[384,256]{1,0:T(8,128)(2,1)} %param.8) | copy-start | bytes 589828
  36.0 10.1 %collective-permute-start = (bf16[192,256]{1,0:T(8,128)(2,1)S(1)}, bf16[192,256]{1,0:T(8,128)(2,1)S(1)}, u32[]{:S(2)}, u32[]{:S(2)}) collective-permute-start(bf16[192,256]{1,0:T(8,128)(2,1)S(1)} %slice.6), channel_id=1, source_target_pairs={{0,1},{1,2},{2,3},{3,4},{4,5},{5,6},{6,7},{7,8},{8,9},{9,10},{10,1... | collective-permute-start | bytes 294920 | tf_op jit(solution)/shard_map/ppermute | solution.py:10
  46.1 24.2 %collective-permute-start.1 = (bf16[384,256]{1,0:T(8,128)(2,1)S(1)}, bf16[384,256]{1,0:T(8,128)(2,1)S(1)}, u32[]{:S(2)}, u32[]{:S(2)}) collective-permute-start(bf16[384,256]{1,0:T(8,128)(2,1)S(1)} %copy-done.3), channel_id=1, source_target_pairs={{0,2},{1,3},{2,4},{3,5},{4,6},{5,7},{6,8},{7,9},{8,10},{9,11},{10,... | collective-permute-start | bytes 589832 | tf_op jit(solution)/shard_map/ppermute | solution.py:10
  49.4 21.6 %collective-permute-start.2 = (bf16[384,256]{1,0:T(8,128)(2,1)S(1)}, bf16[384,256]{1,0:T(8,128)(2,1)}, u32[]{:S(2)}, u32[]{:S(2)}) collective-permute-start(bf16[384,256]{1,0:T(8,128)(2,1)S(1)} %copy-done.3), channel_id=1, source_target_pairs={{0,4},{1,5},{2,6},{3,7},{4,8},{5,9},{6,10},{7,11},{8,12},{9,13},{1... | collective-permute-start | bytes 589832 | tf_op jit(solution)/shard_map/ppermute | solution.py:10
  51.4 21.3 %collective-permute-start.3 = (bf16[384,256]{1,0:T(8,128)(2,1)S(1)}, bf16[384,256]{1,0:T(8,128)(2,1)}, u32[]{:S(2)}, u32[]{:S(2)}) collective-permute-start(bf16[384,256]{1,0:T(8,128)(2,1)S(1)} %copy-done.3), channel_id=1, source_target_pairs={{0,8},{1,9},{2,10},{3,11},{4,12},{5,13},{6,14},{7,15},{8,16},{9,17... | collective-permute-start | bytes 589832 | tf_op jit(solution)/shard_map/ppermute | solution.py:10
  53.3 20.9 %collective-permute-start.4 = (bf16[384,256]{1,0:T(8,128)(2,1)S(1)}, bf16[384,256]{1,0:T(8,128)(2,1)}, u32[]{:S(2)}, u32[]{:S(2)}) collective-permute-start(bf16[384,256]{1,0:T(8,128)(2,1)S(1)} %copy-done.3), channel_id=1, source_target_pairs={{0,16},{1,17},{2,18},{3,19},{4,20},{5,21},{6,22},{7,23},{8,24},{9,... | collective-permute-start | bytes 589832 | tf_op jit(solution)/shard_map/ppermute | solution.py:10
  84.4 1.2 copy-start
  93.6 1.2 copy-start
  102.8 1.2 copy-start
  112.0 1.2 copy-start
  121.2 1.2 copy-start
  130.4 1.2 copy-start
  139.6 1.2 copy-start
  148.8 1.2 copy-start
where the time goes:
time: 160 us; the launch traced here: 157 us
  waiting for transfers between devices  34 us (21%)
  loops' own time  31.4 us (20%)
  starting transfers between devices  28.8 us (18%)
  local copies, waits for them, and re-layouts  28.5 us (18%)
  matrix products  26.9 us (17%)
  other arithmetic  7.38 us (5%)
    ppermute x10, waiting for transfers between devices, from_behind(): return lax.ppermute(block, axis, route)  34 us
    another operation x1, loops' own time, on_device(): attended = lax.map(one_head, jnp.arange(heads, dtype=jnp.int32))  31.4 us
    ppermute x10, starting transfers between devices, from_behind(): return lax.ppermute(block, axis, route)  28.8 us
    dot_general x8, matrix products, one_head(): lax.dot_general(query_one, key_one, (((1,), (1,)), ((), ())), preferred_e...  12.9 us
    dot_general x8, matrix products, one_head(): jnp.dot(weights.astype(jnp.bfloat16), value_one, preferred_element_type=j...  8.57 us
    unnamed x21, local copies, waits for them, and re-layouts  7.71 us
    reduce_sum x8, other arithmetic, one_head(): totals = jnp.sum(weights, axis=-1, keepdims=True)  7.09 us
    dynamic_update_slice x16, local copies, waits for them, and re-layouts, on_device(): attended = lax.map(one_head, jnp.arange(heads, dtype=jnp.int32))  6.23 us
  transfers between devices with their start and end apart: 10, of which 3 were waited for; matrix products, arithmetic and copies ran while one was open for 7% of the time, Pallas kernels for 0%

commit v1 on v0

v1 whole, which is shorter than its diff:
```python
import functools
import math

import jax
import jax.numpy as jnp
from jax import lax
from jax.experimental import pallas as pl
from jax.experimental.pallas import tpu as pltpu
from jax.sharding import PartitionSpec as P

HEAD = 128
STRIP = 128
FAR = (2, 4, 8, 16)
LOW = -1e30
SCALE = math.log2(math.e) / math.sqrt(HEAD)
LIMIT = 40 * 1024 * 1024
VMEM = pl.BlockSpec(memory_space=pltpu.VMEM)
ANY = pl.BlockSpec(memory_space=pl.ANY)


def shifted(block, distance):
    devices = lax.axis_size("seq")
    return lax.ppermute(block, "seq", [(i, (i + distance) % devices) for i in range(devices)])


def pack_kernel(keys, values, both, tail):
    rows, width = keys.shape
    reach = rows - tail.shape[0]
    both[:, :width] = keys[...]
    both[:, width:] = values[...]
    tail[:, :width] = keys[reach:]
    tail[:, width:] = values[reach:]


def pack(keys, values):
    rows, width = keys.shape
    return pl.pallas_call(
        pack_kernel,
        out_shape=(
            jax.ShapeDtypeStruct((rows, 2 * width), keys.dtype),
            jax.ShapeDtypeStruct((rows // 2, 2 * width), keys.dtype),
        ),
        in_specs=[VMEM] * 2,
        out_specs=(VMEM, VMEM),
        name="pack",
    )(keys, values)


def tiles_of(rows, kv_heads):
    return [(g, j) for g in range(kv_heads) for j in range(rows // STRIP)]


def query_tile(queries, g, j, group):
    rows = slice(j * STRIP, (j + 1) * STRIP)
    return jnp.concatenate(
        [queries[rows, (g * group + h) * HEAD : (g * group + h + 1) * HEAD] for h in range(group)],
        axis=0,
    )


def scores_of(key_rows, query):
    return lax.dot_general(
        key_rows, query, (((1,), (1,)), ((), ())), preferred_element_type=jnp.float32
    )


def summed_of(value_rows, weights):
    return lax.dot_general(
        value_rows,
        weights.astype(jnp.bfloat16),
        (((0,), (0,)), ((), ())),
        preferred_element_type=jnp.float32,
    )


def near_kernel(queries, both, tail, acc, stats, joined):
    rows, width = queries.shape
    kv_width = both.shape[1] // 2
    kv_heads = kv_width // HEAD
    group = width // HEAD // kv_heads
    reach = tail.shape[0]
    me = lax.axis_index("seq")
    joined[:reach] = tail[...]
    joined[reach:] = both[...]
    span = reach + STRIP
    columns = group * STRIP
    key_at = lax.broadcasted_iota(jnp.int32, (span, columns), 0)
    row_at = lax.broadcasted_iota(jnp.int32, (1, columns), 1) % STRIP
    for t, (g, j) in enumerate(tiles_of(rows, kv_heads)):
        first = j * STRIP
        key_rows = joined[first : first + span, g * HEAD : (g + 1) * HEAD]
        value_rows = joined[first : first + span, kv_width + g * HEAD : kv_width + (g + 1) * HEAD]
        scores = scores_of(key_rows, query_tile(queries, g, j, group))
        least = jnp.where(me >= 1, 0, max(reach - first, 0))
        allowed = (key_at >= jnp.maximum(row_at, least)) & (key_at <= row_at + reach)
        scores = jnp.where(allowed, scores, LOW)
        top = jnp.max(scores, axis=0, keepdims=True)
        weights = jnp.exp2(scores * SCALE - top * SCALE)
        stats[t : t + 1] = top
        stats[8 + t : 9 + t] = jnp.sum(weights, axis=0, keepdims=True)
        acc[t] = summed_of(value_rows, weights)


def far_step(queries, parts, top, total, acc, g, j, kv_width, group, me):
    query = query_tile(queries, g, j, group)
    scores = []
    for ref, distance in parts:
        part = scores_of(ref[:, g * HEAD : (g + 1) * HEAD], query)
        if me is not None:
            part = jnp.where(me >= distance, part, LOW)
        scores.append(part)
    new_top = top
    for part in scores:
        new_top = jnp.maximum(new_top, jnp.max(part, axis=0, keepdims=True))
    fade = jnp.exp2((top - new_top) * SCALE)
    total = total * fade
    acc = acc * fade
    for part, (ref, _) in zip(scores, parts):
        weights = jnp.exp2(part * SCALE - new_top * SCALE)
        total = total + jnp.sum(weights, axis=0, keepdims=True)
        value_rows = ref[:, kv_width + g * HEAD : kv_width + (g + 1) * HEAD]
        acc = acc + summed_of(value_rows, weights)
    return new_top, total, acc


def with_or_without_mask(distances, body):
    me = lax.axis_index("seq")
    far = max(distances)

    @pl.when(me >= far)
    def _():
        body(None)

    @pl.when(me < far)
    def _():
        body(me)


def far_kernel(distances, queries, acc_in, stats_in, *refs):
    parts = list(zip(refs[: len(distances)], distances))
    acc, stats = refs[len(distances) :]
    rows, width = queries.shape
    kv_width = parts[0][0].shape[1] // 2
    kv_heads = kv_width // HEAD
    group = width // HEAD // kv_heads

    def body(me):
        for t, (g, j) in enumerate(tiles_of(rows, kv_heads)):
            top, total, summed = far_step(
                queries, parts, stats_in[t : t + 1], stats_in[8 + t : 9 + t], acc_in[t],
                g, j, kv_width, group, me,
            )
            stats[t : t + 1] = top
            stats[8 + t : 9 + t] = total
            acc[t] = summed

    with_or_without_mask(distances, body)


def last_kernel(distances, queries, acc_in, stats_in, *refs):
    parts = list(zip(refs[: len(distances)], distances))
    weight_hbm, out_hbm, weight, attended, staged, in_sems, out_sems = refs[len(distances) :]
    rows, width = queries.shape
    kv_width = parts[0][0].shape[1] // 2
    kv_heads = kv_width // HEAD
    group = width // HEAD // kv_heads
    pieces, _, piece = staged.shape

    def fetch(n):
        columns = pl.ds(n * piece, piece)
        return pltpu.make_async_copy(weight_hbm.at[:, columns], weight.at[:, columns], in_sems.at[n])

    def put(n):
        return pltpu.make_async_copy(staged.at[n], out_hbm.at[:, pl.ds(n * piece, piece)], out_sems.at[n])

    for n in range(pieces):
        fetch(n).start()

    def body(me):
        for t, (g, j) in enumerate(tiles_of(rows, kv_heads)):
            _, total, summed = far_step(
                queries, parts, stats_in[t : t + 1], stats_in[8 + t : 9 + t], acc_in[t],
                g, j, kv_width, group, me,
            )
            done = (summed / total).astype(jnp.bfloat16)
            for h in range(group):
                head = g * group + h
                attended[j * STRIP : (j + 1) * STRIP, head * HEAD : (head + 1) * HEAD] = done[
                    :, h * STRIP : (h + 1) * STRIP
                ].T

    with_or_without_mask(distances, body)
    for n in range(pieces):
        fetch(n).wait()
        staged[n] = jnp.dot(
            attended[...], weight[:, n * piece : (n + 1) * piece], preferred_element_type=jnp.float32
        ).astype(jnp.bfloat16)
        put(n).start()
    for n in range(pieces):
        put(n).wait()


def cost(rows, keys, width, extra=0):
    return pl.CostEstimate(
        flops=4 * rows * keys * width + extra,
        bytes_accessed=4 * rows * width * 2 + 4 * keys * 512,
        transcendentals=rows * keys * width // HEAD,
    )


def near(queries, both, tail):
    rows, width = queries.shape
    strips = rows // STRIP
    kv_heads = both.shape[1] // 2 // HEAD
    columns = width // HEAD // kv_heads * STRIP
    return pl.pallas_call(
        near_kernel,
        out_shape=(
            jax.ShapeDtypeStruct((kv_heads * strips, HEAD, columns), jnp.float32),
            jax.ShapeDtypeStruct((16, columns), jnp.float32),
        ),
        in_specs=[VMEM] * 3,
        out_specs=(VMEM, VMEM),
        scratch_shapes=[pltpu.VMEM((rows + tail.shape[0], both.shape[1]), both.dtype)],
        compiler_params=pltpu.CompilerParams(vmem_limit_bytes=LIMIT),
        cost_estimate=cost(rows, 320, width),
        name="near",
    )(queries, both, tail)


def far(queries, state, blocks, distances):
    rows, width = queries.shape
    acc, stats = state
    return pl.pallas_call(
        functools.partial(far_kernel, distances),
        out_shape=tuple(jax.ShapeDtypeStruct(x.shape, x.dtype) for x in state),
        in_specs=[VMEM] * (3 + len(blocks)),
        out_specs=(VMEM, VMEM),
        compiler_params=pltpu.CompilerParams(vmem_limit_bytes=LIMIT),
        cost_estimate=cost(rows, sum(b.shape[0] for b in blocks), width),
        name="far",
    )(queries, acc, stats, *blocks)


def last(queries, state, blocks, distances, out_weight):
    rows, width = queries.shape
    wide = out_weight.shape[1]
    piece = 512
    acc, stats = state
    return pl.pallas_call(
        functools.partial(last_kernel, distances),
        out_shape=jax.ShapeDtypeStruct((rows, wide), jnp.bfloat16),
        in_specs=[VMEM] * (3 + len(blocks)) + [ANY],
        out_specs=ANY,
        scratch_shapes=[
            pltpu.VMEM(out_weight.shape, jnp.bfloat16),
            pltpu.VMEM((rows, width), jnp.bfloat16),
            pltpu.VMEM((wide // piece, rows, piece), jnp.bfloat16),
            pltpu.SemaphoreType.DMA((wide // piece,)),
            pltpu.SemaphoreType.DMA((wide // piece,)),
        ],
        compiler_params=pltpu.CompilerParams(vmem_limit_bytes=LIMIT),
        cost_estimate=cost(rows, sum(b.shape[0] for b in blocks), width, 2 * rows * width * wide),
        name="last",
    )(queries, acc, stats, *blocks, out_weight)


def on_device(queries, keys, values, out_weight):
    both, tail = pack(keys, values)
    before = shifted(tail, 1)
    behind = shifted(both, 2)
    later = shifted(both, 16)
    eighth = shifted(both, 8)
    fourth = shifted(behind, 2)
    state = near(queries, both, before)
    state = far(queries, state, (behind, later), (2, 16))
    state = far(queries, state, (fourth,), (4,))
    return last(queries, state, (eighth,), (8,), out_weight)


def solution(mesh):
    in_specs = (P("seq", None), P("seq", None), P("seq", None), P())
    return jax.shard_map(
        on_device, mesh=mesh, in_specs=in_specs, out_specs=P("seq", None), check_vma=False
    )
```

time: 160 us -> 81.6 us (0.51); the launches traced: 157 us -> 81.3 us
  loops' own time: 31.4 us -> 0 us
  matrix products: 26.9 us -> 0 us
  local copies, waits for them, and re-layouts: 28.5 us -> 2.14 us
  Pallas kernels: 0 us -> 20 us
  starting transfers between devices: 28.8 us -> 13.5 us
  waiting for transfers between devices: 34 us -> 45.3 us
  other arithmetic: 7.38 us -> 0 us
    another operation x1 -> x0, loops' own time: 31.4 us -> none  [on_device(): attended = lax.map(one_head, jnp.arange(heads, dtype=jnp.int32))]
    dot_general x17 -> x0, matrix products: 26.9 us -> none  [the longest x8 12.9 us: one_head(): lax.dot_general(query_one, key_one, (((1,), (1,)), ((), ())), preferred_e...]
    pallas_call x0 -> x5, Pallas kernels: none -> 20 us  [the longest x2 7.97 us: far(): pl.pallas_call(functools.partial(far_kernel, distances), out_shape=tuple(...]
    ppermute x10 -> x5, starting transfers between devices: 28.8 us -> 13.5 us  [shifted(): lax.ppermute(block, 'seq', [(i, (i + distance) % devices) for i in range(...]
    ppermute x10 -> x5, waiting for transfers between devices: 34 us -> 45.3 us  [shifted(): lax.ppermute(block, 'seq', [(i, (i + distance) % devices) for i in range(...]
    reduce_sum x8 -> x0, other arithmetic: 7.09 us -> none  [one_head(): totals = jnp.sum(weights, axis=-1, keepdims=True)]
    dynamic_update_slice x16 -> x0, local copies, waits for them, and re-layouts: 6.23 us -> none  [on_device(): attended = lax.map(one_head, jnp.arange(heads, dtype=jnp.int32))]
    unnamed x21 -> x8, local copies, waits for them, and re-layouts: 7.71 us -> 2.14 us
  transfers between devices with their start and end apart: 10 -> 5, of which waited for: 3 -> 2; matrix products, arithmetic and copies ran while one was open for 7% -> 0% of each run, Pallas kernels for 0% -> 13%
where the time goes in v1:
time: 81.6 us; the launch traced here: 81.3 us
  waiting for transfers between devices  45.3 us (56%)
  Pallas kernels  20 us (25%)
  starting transfers between devices  13.5 us (17%)
  local copies, waits for them, and re-layouts  2.14 us (3%)
    ppermute x5, waiting for transfers between devices, shifted(): lax.ppermute(block, 'seq', [(i, (i + distance) % devices) for i in range(...  45.3 us
    ppermute x5, starting transfers between devices, shifted(): lax.ppermute(block, 'seq', [(i, (i + distance) % devices) for i in range(...  13.5 us
    pallas_call x2, Pallas kernels, far(): pl.pallas_call(functools.partial(far_kernel, distances), out_shape=tuple(...  7.97 us
    pallas_call x1, Pallas kernels, last(): pl.pallas_call(functools.partial(last_kernel, distances), out_shape=jax.S...  7.33 us
    pallas_call x1, Pallas kernels, near(): pl.pallas_call(near_kernel, out_shape=(jax.ShapeDtypeStruct((kv_heads * s...  2.86 us
    unnamed x8, local copies, waits for them, and re-layouts  2.14 us
    pallas_call x1, Pallas kernels, pack(): pl.pallas_call(pack_kernel, out_shape=(jax.ShapeDtypeStruct((rows, 2 * wi...  1.88 us
  transfers between devices with their start and end apart: 5, of which 2 were waited for; matrix products, arithmetic and copies ran while one was open for 0% of the time, Pallas kernels for 13%

profile of v1, /device:TPU:6, one launch (start us, length us, event | category | flops | bytes accessed | tf_op | source)
XLA Modules:
  0.0 81.3 jit_solution(3364280902862114181)
XLA Ops:
  0.0 1.9 %pack.1 = (bf16[384,512]{1,0:T(8,128)(2,1)}, bf16[192,512]{1,0:T(8,128)(2,1)}) custom-call(bf16[384,256]{1,0:T(8,128)(2,1)} %keys.1, bf16[384,256]{1,0:T(8,128)(2,1)} %values.1), custom_call_target="tpu_custom_call" | custom-call | tf_op jit(solution)/shard_map/pack/pallas_call | solution.py:37
  1.9 3.5 %collective-permute-start.1 = (bf16[384,512]{1,0:T(8,128)(2,1)}, bf16[384,512]{1,0:T(8,128)(2,1)S(1)}, u32[]{:S(2)}, u32[]{:S(2)}) collective-permute-start(bf16[384,512]{1,0:T(8,128)(2,1)} %get-tuple-element.13.both), channel_id=1, source_target_pairs={{0,2},{1,3},{2,4},{3,5},{4,6},{5,7},{6,8},{7,9},{8,10},{9,11},{10,... | collective-permute-start | bytes 1179656 | tf_op jit(solution)/shard_map/ppermute | solution.py:23
  5.4 4.3 %collective-permute-start.2 = (bf16[384,512]{1,0:T(8,128)(2,1)}, bf16[384,512]{1,0:T(8,128)(2,1)S(1)}, u32[]{:S(2)}, u32[]{:S(2)}) collective-permute-start(bf16[384,512]{1,0:T(8,128)(2,1)} %get-tuple-element.13.both), channel_id=1, source_target_pairs={{0,16},{1,17},{2,18},{3,19},{4,20},{5,21},{6,22},{7,23},{8,24},{9,... | collective-permute-start | bytes 1179656 | tf_op jit(solution)/shard_map/ppermute | solution.py:23
  9.6 15.8 %collective-permute-done.1.refs_0_ = bf16[384,512]{1,0:T(8,128)(2,1)S(1)} collective-permute-done((bf16[384,512]{1,0:T(8,128)(2,1)}, bf16[384,512]{1,0:T(8,128)(2,1)S(1)}, u32[]{:S(2)}, u32[]{:S(2)}) %collective-permute-start.1) | collective-permute-done | bytes 393248 | tf_op jit(solution)/shard_map/ppermute | solution.py:23
  25.4 1.9 %collective-permute-start.3 = (bf16[384,512]{1,0:T(8,128)(2,1)S(1)}, bf16[384,512]{1,0:T(8,128)(2,1)S(1)}, u32[]{:S(2)}, u32[]{:S(2)}) collective-permute-start(bf16[384,512]{1,0:T(8,128)(2,1)S(1)} %collective-permute-done.1.refs_0_), channel_id=1, source_target_pairs={{0,2},{1,3},{2,4},{3,5},{4,6},{5,7},{6,8},{7,9},{8,10},{9,11},{10,... | collective-permute-start | bytes 1179656 | tf_op jit(solution)/shard_map/ppermute | solution.py:23
  27.3 1.9 %collective-permute-start = (bf16[192,512]{1,0:T(8,128)(2,1)}, bf16[192,512]{1,0:T(8,128)(2,1)S(1)}, u32[]{:S(2)}, u32[]{:S(2)}) collective-permute-start(bf16[192,512]{1,0:T(8,128)(2,1)} %get-tuple-element.14), channel_id=1, source_target_pairs={{0,1},{1,2},{2,3},{3,4},{4,5},{5,6},{6,7},{7,8},{8,9},{9,10},{10,1... | collective-permute-start | bytes 589832 | tf_op jit(solution)/shard_map/ppermute | solution.py:23
  29.2 1.9 %collective-permute-start.4 = (bf16[384,512]{1,0:T(8,128)(2,1)}, bf16[384,512]{1,0:T(8,128)(2,1)S(1)}, u32[]{:S(2)}, u32[]{:S(2)}) collective-permute-start(bf16[384,512]{1,0:T(8,128)(2,1)} %get-tuple-element.13.both), channel_id=1, source_target_pairs={{0,8},{1,9},{2,10},{3,11},{4,12},{5,13},{6,14},{7,15},{8,16},{9,17... | collective-permute-start | bytes 1179656 | tf_op jit(solution)/shard_map/ppermute | solution.py:23
  31.2 29.6 %collective-permute-done.tail = bf16[192,512]{1,0:T(8,128)(2,1)S(1)} collective-permute-done((bf16[192,512]{1,0:T(8,128)(2,1)}, bf16[192,512]{1,0:T(8,128)(2,1)S(1)}, u32[]{:S(2)}, u32[]{:S(2)}) %collective-permute-start) | collective-permute-done | bytes 196640 | tf_op jit(solution)/shard_map/ppermute | solution.py:23
  60.7 0.0 copy-start.1
  60.7 1.1 %copy-done.1 = bf16[384,1024]{1,0:T(8,128)(2,1)S(1)} copy-done((bf16[384,1024]{1,0:T(8,128)(2,1)S(1)}, bf16[384,1024]{1,0:T(8,128)(2,1)}, u32[]{:S(2)}) %copy-start.1) | copy-done | bytes 786456
  61.9 0.0 copy-start.3
  61.9 1.0 %copy-done.3 = bf16[384,512]{1,0:T(8,128)(2,1)S(1)} copy-done((bf16[384,512]{1,0:T(8,128)(2,1)S(1)}, bf16[384,512]{1,0:T(8,128)(2,1)}, u32[]{:S(2)}) %copy-start.3) | copy-done | bytes 393240
  62.9 0.0 copy-start.2
  62.9 2.9 %near.1 = (f32[6,128,512]{2,1,0:T(8,128)S(1)}, f32[16,512]{1,0:T(8,128)S(1)}) custom-call(bf16[384,1024]{1,0:T(8,128)(2,1)S(1)} %copy-done.1, bf16[384,512]{1,0:T(8,128)(2,1)S(1)} %copy-done.3, bf16[192,512]{1,0:T(8,128)(2,1)S(1)} %collective-permute-done.tail), custom_call_target="tpu_custom_call" | custom-call | flops 503316480 | bytes 3801088 | tf_op jit(solution)/shard_map/near/pallas_call | solution.py:216
  65.7 0.0 collective-permute-done.2.refs_1_
  65.8 0.0 copy-done.2
  65.8 0.0 copy-start
  65.8 4.7 %far.2 = (f32[6,128,512]{2,1,0:T(8,128)S(1)}, f32[16,512]{1,0:T(8,128)S(1)}) custom-call(bf16[384,1024]{1,0:T(8,128)(2,1)S(1)} %copy-done.2, f32[6,128,512]{2,1,0:T(8,128)S(1)} %get-tuple-element.15.acc_in, f32[16,512]{1,0:T(8,128)S(1)} %get-tuple-element.16.stats_in, bf16[384,512]{1,0:T(8,128)(2,1)S(1)} %collective-permute-done.1.refs_0_, ...), custom_call_target="tpu_custom_call" | custom-call | flops 1207959552 | bytes 4718592 | tf_op jit(solution)/shard_map/far/pallas_call | solution.py:234
  70.5 0.0 collective-permute-done.3.refs_0_
  70.5 3.2 %far.3 = (f32[6,128,512]{2,1,0:T(8,128)S(1)}, f32[16,512]{1,0:T(8,128)S(1)}) custom-call(bf16[384,1024]{1,0:T(8,128)(2,1)S(1)} %copy-done.2, f32[6,128,512]{2,1,0:T(8,128)S(1)} %get-tuple-element.17.acc_in, f32[16,512]{1,0:T(8,128)S(1)} %get-tuple-element.18.stats_in, bf16[384,512]{1,0:T(8,128)(2,1)S(1)} %collective-permute-done.3.refs_0_), custom_call_target="tpu_custom_call" | custom-call | flops 603979776 | bytes 3932160 | tf_op jit(solution)/shard_map/far/pallas_call | solution.py:234
  73.8 0.0 collective-permute-done.4.refs_0_
  73.8 0.0 copy-done
  73.8 7.3 %last.1 = bf16[384,2048]{1,0:T(8,128)(2,1)} custom-call(bf16[384,1024]{1,0:T(8,128)(2,1)S(1)} %copy-done.2, f32[6,128,512]{2,1,0:T(8,128)S(1)} %get-tuple-element.19.acc_in, f32[16,512]{1,0:T(8,128)S(1)} %get-tuple-element.20.stats_in, bf16[384,512]{1,0:T(8,128)(2,1)S(1)} %collective-permute-done.4.refs_0_, bf16[1024,2048]{1,0:T(8,128)(2,1)S(1)} %copy-done), custom_call_target="tpu_custom_call" | custom-call | flops 2214592512 | bytes 3932160 | tf_op jit(solution)/shard_map/last/pallas_call | solution.py:250
Async XLA Ops:
  1.9 23.5 %collective-permute-start.1 = (bf16[384,512]{1,0:T(8,128)(2,1)}, bf16[384,512]{1,0:T(8,128)(2,1)S(1)}, u32[]{:S(2)}, u32[]{:S(2)}) collective-permute-start(bf16[384,512]{1,0:T(8,128)(2,1)} %get-tuple-element.13.both), channel_id=1, source_target_pairs={{0,2},{1,3},{2,4},{3,5},{4,6},{5,7},{6,8},{7,9},{8,10},{9,11},{10,... | collective-permute-start | bytes 1179656 | tf_op jit(solution)/shard_map/ppermute | solution.py:23
  5.4 60.4 %collective-permute-start.2 = (bf16[384,512]{1,0:T(8,128)(2,1)}, bf16[384,512]{1,0:T(8,128)(2,1)S(1)}, u32[]{:S(2)}, u32[]{:S(2)}) collective-permute-start(bf16[384,512]{1,0:T(8,128)(2,1)} %get-tuple-element.13.both), channel_id=1, source_target_pairs={{0,16},{1,17},{2,18},{3,19},{4,20},{5,21},{6,22},{7,23},{8,24},{9,... | collective-permute-start | bytes 1179656 | tf_op jit(solution)/shard_map/ppermute | solution.py:23
  25.4 45.1 %collective-permute-start.3 = (bf16[384,512]{1,0:T(8,128)(2,1)S(1)}, bf16[384,512]{1,0:T(8,128)(2,1)S(1)}, u32[]{:S(2)}, u32[]{:S(2)}) collective-permute-start(bf16[384,512]{1,0:T(8,128)(2,1)S(1)} %collective-permute-done.1.refs_0_), channel_id=1, source_target_pairs={{0,2},{1,3},{2,4},{3,5},{4,6},{5,7},{6,8},{7,9},{8,10},{9,11},{10,... | collective-permute-start | bytes 1179656 | tf_op jit(solution)/shard_map/ppermute | solution.py:23
  27.3 33.4 %collective-permute-start = (bf16[192,512]{1,0:T(8,128)(2,1)}, bf16[192,512]{1,0:T(8,128)(2,1)S(1)}, u32[]{:S(2)}, u32[]{:S(2)}) collective-permute-start(bf16[192,512]{1,0:T(8,128)(2,1)} %get-tuple-element.14), channel_id=1, source_target_pairs={{0,1},{1,2},{2,3},{3,4},{4,5},{5,6},{6,7},{7,8},{8,9},{9,10},{10,1... | collective-permute-start | bytes 589832 | tf_op jit(solution)/shard_map/ppermute | solution.py:23
  29.2 44.5 %collective-permute-start.4 = (bf16[384,512]{1,0:T(8,128)(2,1)}, bf16[384,512]{1,0:T(8,128)(2,1)S(1)}, u32[]{:S(2)}, u32[]{:S(2)}) collective-permute-start(bf16[384,512]{1,0:T(8,128)(2,1)} %get-tuple-element.13.both), channel_id=1, source_target_pairs={{0,8},{1,9},{2,10},{3,11},{4,12},{5,13},{6,14},{7,15},{8,16},{9,17... | collective-permute-start | bytes 1179656 | tf_op jit(solution)/shard_map/ppermute | solution.py:23
  60.7 1.1 %copy-start.1 = (bf16[384,1024]{1,0:T(8,128)(2,1)S(1)}, bf16[384,1024]{1,0:T(8,128)(2,1)}, u32[]{:S(2)}) copy-start(bf16[384,1024]{1,0:T(8,128)(2,1)} %queries.7) | copy-start | bytes 2359300
  61.9 1.0 %copy-start.3 = (bf16[384,512]{1,0:T(8,128)(2,1)S(1)}, bf16[384,512]{1,0:T(8,128)(2,1)}, u32[]{:S(2)}) copy-start(bf16[384,512]{1,0:T(8,128)(2,1)} %get-tuple-element.13.both) | copy-start | bytes 1179652
  62.9 2.9 %copy-start.2 = (bf16[384,1024]{1,0:T(8,128)(2,1)S(1)}, bf16[384,1024]{1,0:T(8,128)(2,1)}, u32[]{:S(2)}) copy-start(bf16[384,1024]{1,0:T(8,128)(2,1)} %queries.7) | copy-start | bytes 2359300
  65.8 8.0 %copy-start = (bf16[1024,2048]{1,0:T(8,128)(2,1)S(1)}, bf16[1024,2048]{1,0:T(8,128)(2,1)}, u32[]{:S(2)}) copy-start(bf16[1024,2048]{1,0:T(8,128)(2,1)} %refs_1_.1) | copy-start | bytes 12582916

commit v2 on v1

v2 whole, which is shorter than its diff:
```python
import functools
import math

import jax
import jax.numpy as jnp
from jax import lax
from jax.experimental import pallas as pl
from jax.experimental.pallas import tpu as pltpu
from jax.sharding import PartitionSpec as P

HEAD = 128
STRIP = 128
RING = 8
LOW = -1e30
MOST = 2.0**80
SCALE = math.log2(math.e) / math.sqrt(HEAD)
LIMIT = 36 * 1024 * 1024
VMEM = pl.BlockSpec(memory_space=pltpu.VMEM)
ANY = pl.BlockSpec(memory_space=pl.ANY)


def shifted(block, distance):
    devices = lax.axis_size("seq")
    return lax.ppermute(block, "seq", [(i, (i + distance) % devices) for i in range(devices)])


def routed(block, target):
    chips = lax.axis_size("seq") // 2
    routes = [(2 * c + k, 2 * (target(c) % chips) + k) for c in range(chips) for k in range(2)]
    return lax.ppermute(block, "seq", routes)


def back(c, hops):
    return c - hops if c % RING >= hops else c - hops + RING


def from_back(c, hops):
    return (c + hops if c % RING + hops < RING else c + hops - RING) + 4


def pack_kernel(keys, values, both, tail, *rest):
    *halves, sems = rest
    rows, width = keys.shape
    copies = [
        pltpu.make_async_copy(source, both.at[:, pl.ds(n * width, width)], sems.at[n])
        for n, source in enumerate((keys, values))
    ]
    for copy in copies:
        copy.start()
    for copy in copies:
        copy.wait()
    tail[...] = both[rows - tail.shape[0] :]
    first = 0
    for half in halves:
        half[...] = both[first : first + half.shape[0]]
        first += half.shape[0]


def pack(keys, values, split=None):
    rows, width = keys.shape
    counts = [rows, rows // 2] + ([split, rows - split] if split else [])
    return pl.pallas_call(
        pack_kernel,
        out_shape=tuple(jax.ShapeDtypeStruct((n, 2 * width), keys.dtype) for n in counts),
        in_specs=[pl.BlockSpec(memory_space=pltpu.HBM)] * 2,
        out_specs=(VMEM,) * len(counts),
        scratch_shapes=[pltpu.SemaphoreType.DMA((2,))],
        compiler_params=pltpu.CompilerParams(vmem_limit_bytes=8 * 1024 * 1024),
        name="pack",
    )(keys, values)


def tiles_of(rows, kv_heads):
    return [(g, j) for g in range(kv_heads) for j in range(rows // STRIP)]


def query_tile(queries, g, j, group):
    rows = slice(j * STRIP, (j + 1) * STRIP)
    return jnp.concatenate(
        [queries[rows, (g * group + h) * HEAD : (g * group + h + 1) * HEAD] for h in range(group)],
        axis=0,
    )


def scores_of(key_rows, query):
    return lax.dot_general(
        key_rows, query, (((1,), (1,)), ((), ())), preferred_element_type=jnp.float32
    )


def summed_of(value_rows, weights):
    return lax.dot_general(
        value_rows,
        weights.astype(jnp.bfloat16),
        (((0,), (0,)), ((), ())),
        preferred_element_type=jnp.float32,
    )


def sizes_of(queries, kv_width):
    width = queries.shape[1]
    kv_heads = kv_width // HEAD
    return kv_heads, width // HEAD // kv_heads


def in_turn(tiles, ahead, finish):
    scores = ahead(0, *tiles[0])
    for t, (g, j) in enumerate(tiles):
        later = ahead(t + 1, *tiles[t + 1]) if t + 1 < len(tiles) else None
        finish(t, g, j, scores)
        scores = later


def near_kernel(queries, both, tail, acc, stats, joined):
    rows = queries.shape[0]
    kv_width = both.shape[1] // 2
    kv_heads, group = sizes_of(queries, kv_width)
    reach = tail.shape[0]
    me = lax.axis_index("seq")
    joined[:reach] = tail[...]
    joined[reach:] = both[...]
    span = reach + STRIP
    columns = group * STRIP
    key_at = lax.broadcasted_iota(jnp.int32, (span, columns), 0)
    row_at = lax.broadcasted_iota(jnp.int32, (1, columns), 1) % STRIP

    def ahead(t, g, j):
        key_rows = joined[j * STRIP : j * STRIP + span, g * HEAD : (g + 1) * HEAD]
        return scores_of(key_rows, query_tile(queries, g, j, group))

    def finish(t, g, j, scores):
        first = j * STRIP
        value_rows = joined[first : first + span, kv_width + g * HEAD : kv_width + (g + 1) * HEAD]
        least = jnp.where(me >= 1, 0, max(reach - first, 0))
        allowed = (key_at >= jnp.maximum(row_at, least)) & (key_at <= row_at + reach)
        scores = jnp.where(allowed, scores, LOW)
        top = jnp.max(scores, axis=0, keepdims=True)
        weights = jnp.exp2(scores * SCALE - top * SCALE)
        stats[t : t + 1] = top
        stats[8 + t : 9 + t] = jnp.sum(weights, axis=0, keepdims=True)
        acc[t] = summed_of(value_rows, weights)

    in_turn(tiles_of(rows, kv_heads), ahead, finish)


def add_parts(queries, pieces, acc_in, stats_in, acc, stats, flag):
    rows = queries.shape[0]
    kv_width = pieces[0][0].shape[1] // 2
    kv_heads, group = sizes_of(queries, kv_width)
    tiles = tiles_of(rows, kv_heads)
    me = lax.axis_index("seq")
    flag[0] = 0

    def scores_with(parts, g, j):
        query = query_tile(queries, g, j, group)
        return [scores_of(ref[:, g * HEAD : (g + 1) * HEAD], query) for ref, _ in parts]

    def values_of(ref, g):
        return ref[:, kv_width + g * HEAD : kv_width + (g + 1) * HEAD]

    def same_top(parts):
        largest = []

        def finish(t, g, j, scores):
            top = stats_in[t : t + 1]
            total = stats_in[8 + t : 9 + t]
            summed = acc_in[t]
            for part, (ref, _) in zip(scores, parts):
                weights = jnp.exp2(part * SCALE - top * SCALE)
                total = total + jnp.sum(weights, axis=0, keepdims=True)
                summed = summed + summed_of(values_of(ref, g), weights)
            stats[t : t + 1] = top
            stats[8 + t : 9 + t] = total
            acc[t] = summed
            largest.append(total)

        in_turn(tiles, lambda t, g, j: scores_with(parts, g, j), finish)
        most = jnp.max(functools.reduce(jnp.maximum, largest))
        flag[0] = jnp.where(most < MOST, 0, 1)

    def new_top():
        def one(t, g, j):
            scores = [
                jnp.where(me >= distance, part, LOW)
                for part, (_, distance) in zip(scores_with(pieces, g, j), pieces)
            ]
            old = stats_in[t : t + 1]
            top = old
            for part in scores:
                top = jnp.maximum(top, jnp.max(part, axis=0, keepdims=True))
            fade = jnp.exp2(old * SCALE - top * SCALE)
            total = stats_in[8 + t : 9 + t] * fade
            summed = acc_in[t] * fade
            for part, (ref, _) in zip(scores, pieces):
                weights = jnp.exp2(part * SCALE - top * SCALE)
                total = total + jnp.sum(weights, axis=0, keepdims=True)
                summed = summed + summed_of(values_of(ref, g), weights)
            stats[t : t + 1] = top
            stats[8 + t : 9 + t] = total
            acc[t] = summed

        for t, (g, j) in enumerate(tiles):
            one(t, g, j)

    bounds = sorted({distance for _, distance in pieces})

    @pl.when(me < bounds[0])
    def _():
        acc[...] = acc_in[...]
        stats[...] = stats_in[...]

    for low, high in zip(bounds, bounds[1:] + [None]):
        here = me >= low if high is None else (me >= low) & (me < high)

        @pl.when(here)
        def _(low=low):
            same_top([(ref, distance) for ref, distance in pieces if distance <= low])

    @pl.when(flag[0] == 1)
    def _():
        new_top()


def far_kernel(distances, queries, acc_in, stats_in, *refs):
    pieces = list(zip(refs[: len(distances)], distances))
    acc, stats, flag = refs[len(distances) :]
    add_parts(queries, pieces, acc_in, stats_in, acc, stats, flag)


def last_kernel(distances, queries, acc_in, stats_in, *refs):
    pieces = list(zip(refs[: len(distances)], distances))
    weight, out_hbm, acc, stats, flag, attended, staged, sems = refs[len(distances) :]
    rows = queries.shape[0]
    kv_heads, group = sizes_of(queries, pieces[0][0].shape[1] // 2)
    cuts, _, cut = staged.shape
    add_parts(queries, pieces, acc_in, stats_in, acc, stats, flag)
    for t, (g, j) in enumerate(tiles_of(rows, kv_heads)):
        done = (acc[t] / stats[8 + t : 9 + t]).astype(jnp.bfloat16)
        for h in range(group):
            head = g * group + h
            attended[j * STRIP : (j + 1) * STRIP, head * HEAD : (head + 1) * HEAD] = done[
                :, h * STRIP : (h + 1) * STRIP
            ].T

    def put(n):
        return pltpu.make_async_copy(staged.at[n], out_hbm.at[:, pl.ds(n * cut, cut)], sems.at[n])

    for n in range(cuts):
        staged[n] = jnp.dot(
            attended[...], weight[:, n * cut : (n + 1) * cut], preferred_element_type=jnp.float32
        ).astype(jnp.bfloat16)
        put(n).start()
    for n in range(cuts):
        put(n).wait()


def cost(rows, keys, width, extra=0):
    return pl.CostEstimate(
        flops=4 * rows * keys * width + extra,
        bytes_accessed=4 * rows * width * 2 + 4 * keys * 512,
        transcendentals=rows * keys * width // HEAD,
    )


def near(queries, both, tail):
    rows, width = queries.shape
    strips = rows // STRIP
    kv_heads = both.shape[1] // 2 // HEAD
    columns = width // HEAD // kv_heads * STRIP
    return pl.pallas_call(
        near_kernel,
        out_shape=(
            jax.ShapeDtypeStruct((kv_heads * strips, HEAD, columns), jnp.float32),
            jax.ShapeDtypeStruct((16, columns), jnp.float32),
        ),
        in_specs=[VMEM] * 3,
        out_specs=(VMEM, VMEM),
        scratch_shapes=[pltpu.VMEM((rows + tail.shape[0], both.shape[1]), both.dtype)],
        compiler_params=pltpu.CompilerParams(vmem_limit_bytes=LIMIT),
        cost_estimate=cost(rows, 320, width),
        name="near",
    )(queries, both, tail)


def far(queries, state, blocks, distances):
    rows, width = queries.shape
    acc, stats = state
    return pl.pallas_call(
        functools.partial(far_kernel, distances),
        out_shape=tuple(jax.ShapeDtypeStruct(x.shape, x.dtype) for x in state),
        in_specs=[VMEM] * (3 + len(blocks)),
        out_specs=(VMEM, VMEM),
        scratch_shapes=[pltpu.SMEM((1,), jnp.int32)],
        compiler_params=pltpu.CompilerParams(vmem_limit_bytes=LIMIT),
        cost_estimate=cost(rows, sum(b.shape[0] for b in blocks), width),
        name="far",
    )(queries, acc, stats, *blocks)


def last(queries, state, blocks, distances, out_weight):
    rows, width = queries.shape
    wide = out_weight.shape[1]
    cut = 512
    acc, stats = state
    return pl.pallas_call(
        functools.partial(last_kernel, distances),
        out_shape=jax.ShapeDtypeStruct((rows, wide), jnp.bfloat16),
        in_specs=[VMEM] * (4 + len(blocks)),
        out_specs=ANY,
        scratch_shapes=[
            pltpu.VMEM(acc.shape, acc.dtype),
            pltpu.VMEM(stats.shape, stats.dtype),
            pltpu.SMEM((1,), jnp.int32),
            pltpu.VMEM((rows, width), jnp.bfloat16),
            pltpu.VMEM((wide // cut, rows, cut), jnp.bfloat16),
            pltpu.SemaphoreType.DMA((wide // cut,)),
        ],
        compiler_params=pltpu.CompilerParams(vmem_limit_bytes=LIMIT),
        cost_estimate=cost(rows, sum(b.shape[0] for b in blocks), width, 2 * rows * width * wide),
        name="last",
    )(queries, acc, stats, *blocks, out_weight)


def on_device(queries, keys, values, out_weight):
    both, tail, part, rest = pack(keys, values, 192)
    behind = shifted(both, 2)
    part = routed(part, lambda c: back(c, 1))
    before = shifted(tail, 1)
    eighth_rest = shifted(rest, 8)
    later = shifted(both, 16)
    behind, before, part = lax.optimization_barrier((behind, before, part))
    fourth = shifted(behind, 2)
    eighth_first = routed(part, lambda c: from_back(c, 1))
    state = near(queries, both, before)
    state = far(queries, state, (eighth_rest, later), (8, 16))
    state = far(queries, state, (behind, fourth), (2, 4))
    return last(queries, state, (eighth_first,), (8,), out_weight)


def solution(mesh):
    in_specs = (P("seq", None), P("seq", None), P("seq", None), P())
    return jax.shard_map(
        on_device, mesh=mesh, in_specs=in_specs, out_specs=P("seq", None), check_vma=False
    )
```

time: 81.6 us -> 65.8 us (0.81)
  waiting for transfers between devices: 45.3 us -> 21.8 us
  starting transfers between devices: 13.5 us -> 20.8 us
  Pallas kernels: 20 us -> 19 us
  local copies, waits for them, and re-layouts: 2.14 us -> 2.99 us
    ppermute x5, waiting for transfers between devices: 45.3 us -> 21.8 us  [shifted(): lax.ppermute(block, 'seq', [(i, (i + distance) % devices) for i in range(...]
    ppermute x0 -> x2, starting transfers between devices: none -> 7.3 us  [routed(): return lax.ppermute(block, 'seq', routes)]
    pallas_call x2, Pallas kernels: 7.97 us -> 13.1 us  [far(): pl.pallas_call(functools.partial(far_kernel, distances), out_shape=tuple(...]
    pallas_call x1, Pallas kernels: 7.33 us -> 3.66 us  [last(): pl.pallas_call(functools.partial(last_kernel, distances), out_shape=jax.S...]
    pallas_call x1, Pallas kernels: 1.88 us -> 0.09 us  [pack(): pl.pallas_call(pack_kernel, out_shape=tuple((jax.ShapeDtypeStruct((n, 2 *...]
    unnamed x8 -> x10, local copies, waits for them, and re-layouts: 2.14 us -> 2.99 us
  transfers between devices with their start and end apart: 5 -> 7, of which waited for: 2 -> 3; matrix products, arithmetic and copies ran while one was open for 0% -> 0% of each run, Pallas kernels for 13% -> 24%
where the time goes in v2:
time: 65.8 us; the launch traced here: 64.9 us
  waiting for transfers between devices  21.8 us (33%)
  starting transfers between devices  20.8 us (32%)
  Pallas kernels  19 us (29%)
  local copies, waits for them, and re-layouts  2.99 us (5%)
    ppermute x5, waiting for transfers between devices, shifted(): lax.ppermute(block, 'seq', [(i, (i + distance) % devices) for i in range(...  21.8 us
    ppermute x5, starting transfers between devices, shifted(): lax.ppermute(block, 'seq', [(i, (i + distance) % devices) for i in range(...  13.5 us
    pallas_call x2, Pallas kernels, far(): pl.pallas_call(functools.partial(far_kernel, distances), out_shape=tuple(...  13.1 us
    ppermute x2, starting transfers between devices, routed(): return lax.ppermute(block, 'seq', routes)  7.3 us
    pallas_call x1, Pallas kernels, last(): pl.pallas_call(functools.partial(last_kernel, distances), out_shape=jax.S...  3.66 us
    unnamed x10, local copies, waits for them, and re-layouts  2.99 us
    pallas_call x1, Pallas kernels, near(): pl.pallas_call(near_kernel, out_shape=(jax.ShapeDtypeStruct((kv_heads * s...  2.14 us
  transfers between devices with their start and end apart: 7, of which 3 were waited for; matrix products, arithmetic and copies ran while one was open for 0% of the time, Pallas kernels for 24%

profile of v2, /device:TPU:6, one launch (start us, length us, event | category | flops | bytes accessed | tf_op | source)
XLA Modules:
  0.0 64.9 jit_solution(8223813235836547296)
XLA Ops:
  0.0 0.0 copy-start.3
  0.0 0.9 %copy-done.3 = bf16[384,256]{1,0:T(8,128)(2,1)S(1)} copy-done((bf16[384,256]{1,0:T(8,128)(2,1)S(1)}, bf16[384,256]{1,0:T(8,128)(2,1)}, u32[]{:S(2)}) %copy-start.3) | copy-done | bytes 196632
  0.9 0.0 copy-start.4
  0.9 0.9 %copy-done.4 = bf16[384,256]{1,0:T(8,128)(2,1)S(1)} copy-done((bf16[384,256]{1,0:T(8,128)(2,1)S(1)}, bf16[384,256]{1,0:T(8,128)(2,1)}, u32[]{:S(2)}) %copy-start.4) | copy-done | bytes 196632
  1.9 0.1 pack.1
  2.0 3.5 %collective-permute-start = (bf16[384,512]{1,0:T(8,128)(2,1)S(1)}, bf16[384,512]{1,0:T(8,128)(2,1)S(1)}, u32[]{:S(2)}, u32[]{:S(2)}) collective-permute-start(bf16[384,512]{1,0:T(8,128)(2,1)S(1)} %get-tuple-element.18.both), channel_id=1, source_target_pairs={{0,2},{1,3},{2,4},{3,5},{4,6},{5,7},{6,8},{7,9},{8,10},{9,11},{10,... | collective-permute-start | bytes 1179656 | tf_op jit(solution)/shard_map/ppermute | solution.py:24
  5.4 1.9 %collective-permute-start.1 = (bf16[192,512]{1,0:T(8,128)(2,1)S(1)}, bf16[192,512]{1,0:T(8,128)(2,1)S(1)}, u32[]{:S(2)}, u32[]{:S(2)}) collective-permute-start(bf16[192,512]{1,0:T(8,128)(2,1)S(1)} %get-tuple-element.19), channel_id=1, source_target_pairs={{0,1},{1,2},{2,3},{3,4},{4,5},{5,6},{6,7},{7,8},{8,9},{9,10},{10,1... | collective-permute-start | bytes 589832 | tf_op jit(solution)/shard_map/ppermute | solution.py:24
  7.4 5.4 %collective-permute-start.2 = (bf16[192,512]{1,0:T(8,128)(2,1)S(1)}, bf16[192,512]{1,0:T(8,128)(2,1)S(1)}, u32[]{:S(2)}, u32[]{:S(2)}) collective-permute-start(bf16[192,512]{1,0:T(8,128)(2,1)S(1)} %get-tuple-element.20), channel_id=1, source_target_pairs={{0,14},{1,15},{2,0},{3,1},{4,2},{5,3},{6,4},{7,5},{8,6},{9,7},{10,... | collective-permute-start | bytes 589832 | tf_op jit(solution)/shard_map/ppermute | solution.py:30
  12.8 4.3 %collective-permute-start.4 = (bf16[384,512]{1,0:T(8,128)(2,1)S(1)}, bf16[384,512]{1,0:T(8,128)(2,1)S(1)}, u32[]{:S(2)}, u32[]{:S(2)}) collective-permute-start(bf16[384,512]{1,0:T(8,128)(2,1)S(1)} %get-tuple-element.18.both), channel_id=1, source_target_pairs={{0,16},{1,17},{2,18},{3,19},{4,20},{5,21},{6,22},{7,23},{8,24},{9,... | collective-permute-start | bytes 1179656 | tf_op jit(solution)/shard_map/ppermute | solution.py:24
  17.0 10.3 %collective-permute-done.1.tail = bf16[192,512]{1,0:T(8,128)(2,1)S(1)} collective-permute-done((bf16[192,512]{1,0:T(8,128)(2,1)S(1)}, bf16[192,512]{1,0:T(8,128)(2,1)S(1)}, u32[]{:S(2)}, u32[]{:S(2)}) %collective-permute-start.1) | collective-permute-done | bytes 196640 | tf_op jit(solution)/shard_map/ppermute | solution.py:24
  27.4 0.0 collective-permute-done.2
  27.4 0.0 collective-permute-done.refs_0_
  27.4 1.9 %collective-permute-start.5 = (bf16[384,512]{1,0:T(8,128)(2,1)S(1)}, bf16[384,512]{1,0:T(8,128)(2,1)S(1)}, u32[]{:S(2)}, u32[]{:S(2)}) collective-permute-start(bf16[384,512]{1,0:T(8,128)(2,1)S(1)} %collective-permute-done.refs_0_), channel_id=1, source_target_pairs={{0,2},{1,3},{2,4},{3,5},{4,6},{5,7},{6,8},{7,9},{8,10},{9,11},{10,... | collective-permute-start | bytes 1179656 | tf_op jit(solution)/shard_map/ppermute | solution.py:24
  29.3 1.9 %collective-permute-start.3 = (bf16[192,512]{1,0:T(8,128)(2,1)S(1)}, bf16[192,512]{1,0:T(8,128)(2,1)S(1)}, u32[]{:S(2)}, u32[]{:S(2)}) collective-permute-start(bf16[192,512]{1,0:T(8,128)(2,1)S(1)} %get-tuple-element.24), channel_id=1, source_target_pairs={{0,8},{1,9},{2,10},{3,11},{4,12},{5,13},{6,14},{7,15},{8,16},{9,17... | collective-permute-start | bytes 589832 | tf_op jit(solution)/shard_map/ppermute | solution.py:24
  31.2 1.9 %collective-permute-start.6 = (bf16[192,512]{1,0:T(8,128)(2,1)S(1)}, bf16[192,512]{1,0:T(8,128)(2,1)S(1)}, u32[]{:S(2)}, u32[]{:S(2)}) collective-permute-start(bf16[192,512]{1,0:T(8,128)(2,1)S(1)} %collective-permute-done.2), channel_id=1, source_target_pairs={{0,10},{1,11},{2,12},{3,13},{4,14},{5,15},{6,16},{7,17},{8,18},{9,... | collective-permute-start | bytes 589832 | tf_op jit(solution)/shard_map/ppermute | solution.py:30
  33.2 0.0 copy-start.1
  33.2 1.1 %copy-done.1 = bf16[384,1024]{1,0:T(8,128)(2,1)S(1)} copy-done((bf16[384,1024]{1,0:T(8,128)(2,1)S(1)}, bf16[384,1024]{1,0:T(8,128)(2,1)}, u32[]{:S(2)}) %copy-start.1) | copy-done | bytes 786456
  34.3 0.0 copy-start.2
  34.3 2.1 %near.1 = (f32[6,128,512]{2,1,0:T(8,128)S(1)}, f32[16,512]{1,0:T(8,128)S(1)}) custom-call(bf16[384,1024]{1,0:T(8,128)(2,1)S(1)} %copy-done.1, bf16[384,512]{1,0:T(8,128)(2,1)S(1)} %get-tuple-element.18.both, bf16[192,512]{1,0:T(8,128)(2,1)S(1)} %collective-permute-done.1.tail), custom_call_target="tpu_custom_call" | custom-call | flops 503316480 | bytes 3801088 | tf_op jit(solution)/shard_map/near/pallas_call | solution.py:270
  36.5 10.5 %collective-permute-done.3.refs_0_ = bf16[192,512]{1,0:T(8,128)(2,1)S(1)} collective-permute-done((bf16[192,512]{1,0:T(8,128)(2,1)S(1)}, bf16[192,512]{1,0:T(8,128)(2,1)S(1)}, u32[]{:S(2)}, u32[]{:S(2)}) %collective-permute-start.3) | collective-permute-done | bytes 196640 | tf_op jit(solution)/shard_map/ppermute | solution.py:24
  47.0 0.9 %collective-permute-done.4.refs_1_ = bf16[384,512]{1,0:T(8,128)(2,1)S(1)} collective-permute-done((bf16[384,512]{1,0:T(8,128)(2,1)S(1)}, bf16[384,512]{1,0:T(8,128)(2,1)S(1)}, u32[]{:S(2)}, u32[]{:S(2)}) %collective-permute-start.4) | collective-permute-done | bytes 393248 | tf_op jit(solution)/shard_map/ppermute | solution.py:24
  47.9 0.0 copy-done.2
  47.9 5.7 %far.2 = (f32[6,128,512]{2,1,0:T(8,128)S(1)}, f32[16,512]{1,0:T(8,128)S(1)}) custom-call(bf16[384,1024]{1,0:T(8,128)(2,1)S(1)} %copy-done.2, f32[6,128,512]{2,1,0:T(8,128)S(1)} %get-tuple-element.22.acc_in, f32[16,512]{1,0:T(8,128)S(1)} %get-tuple-element.23.stats_in, bf16[192,512]{1,0:T(8,128)(2,1)S(1)} %collective-permute-done.3.refs_0_, ...), custom_call_target="tpu_custom_call" | custom-call | flops 905969664 | bytes 4325376 | tf_op jit(solution)/shard_map/far/pallas_call | solution.py:288
  53.6 0.0 collective-permute-done.5.refs_1_
  53.6 0.0 copy-start
  53.6 7.5 %far.3 = (f32[6,128,512]{2,1,0:T(8,128)S(1)}, f32[16,512]{1,0:T(8,128)S(1)}) custom-call(bf16[384,1024]{1,0:T(8,128)(2,1)S(1)} %copy-done.2, f32[6,128,512]{2,1,0:T(8,128)S(1)} %get-tuple-element.25.acc_in, f32[16,512]{1,0:T(8,128)S(1)} %get-tuple-element.26.stats_in, bf16[384,512]{1,0:T(8,128)(2,1)S(1)} %collective-permute-done.refs_0_, ...), custom_call_target="tpu_custom_call" | custom-call | flops 1207959552 | bytes 4718592 | tf_op jit(solution)/shard_map/far/pallas_call | solution.py:288
  61.1 0.0 collective-permute-done.6.refs_0_
  61.1 0.0 copy-done
  61.1 3.7 %last.1 = bf16[384,2048]{1,0:T(8,128)(2,1)} custom-call(bf16[384,1024]{1,0:T(8,128)(2,1)S(1)} %copy-done.2, f32[6,128,512]{2,1,0:T(8,128)S(1)} %get-tuple-element.28.acc_in, f32[16,512]{1,0:T(8,128)S(1)} %get-tuple-element.29.stats_in, bf16[192,512]{1,0:T(8,128)(2,1)S(1)} %collective-permute-done.6.refs_0_, bf16[1024,2048]{1,0:T(8,128)(2,1)S(1)} %copy-done), custom_call_target="tpu_custom_call" | custom-call | flops 1912602624 | bytes 3538944 | tf_op jit(solution)/shard_map/last/pallas_call | solution.py:305
Async XLA Ops:
  0.0 0.9 %copy-start.3 = (bf16[384,256]{1,0:T(8,128)(2,1)S(1)}, bf16[384,256]{1,0:T(8,128)(2,1)}, u32[]{:S(2)}) copy-start(bf16[384,256]{1,0:T(8,128)(2,1)} %keys.1) | copy-start | bytes 589828
  0.9 0.9 %copy-start.4 = (bf16[384,256]{1,0:T(8,128)(2,1)S(1)}, bf16[384,256]{1,0:T(8,128)(2,1)}, u32[]{:S(2)}) copy-start(bf16[384,256]{1,0:T(8,128)(2,1)} %values.1) | copy-start | bytes 589828
  2.0 25.4 %collective-permute-start = (bf16[384,512]{1,0:T(8,128)(2,1)S(1)}, bf16[384,512]{1,0:T(8,128)(2,1)S(1)}, u32[]{:S(2)}, u32[]{:S(2)}) collective-permute-start(bf16[384,512]{1,0:T(8,128)(2,1)S(1)} %get-tuple-element.18.both), channel_id=1, source_target_pairs={{0,2},{1,3},{2,4},{3,5},{4,6},{5,7},{6,8},{7,9},{8,10},{9,11},{10,... | collective-permute-start | bytes 1179656 | tf_op jit(solution)/shard_map/ppermute | solution.py:24
  5.4 21.9 %collective-permute-start.1 = (bf16[192,512]{1,0:T(8,128)(2,1)S(1)}, bf16[192,512]{1,0:T(8,128)(2,1)S(1)}, u32[]{:S(2)}, u32[]{:S(2)}) collective-permute-start(bf16[192,512]{1,0:T(8,128)(2,1)S(1)} %get-tuple-element.19), channel_id=1, source_target_pairs={{0,1},{1,2},{2,3},{3,4},{4,5},{5,6},{6,7},{7,8},{8,9},{9,10},{10,1... | collective-permute-start | bytes 589832 | tf_op jit(solution)/shard_map/ppermute | solution.py:24
  7.4 20.0 %collective-permute-start.2 = (bf16[192,512]{1,0:T(8,128)(2,1)S(1)}, bf16[192,512]{1,0:T(8,128)(2,1)S(1)}, u32[]{:S(2)}, u32[]{:S(2)}) collective-permute-start(bf16[192,512]{1,0:T(8,128)(2,1)S(1)} %get-tuple-element.20), channel_id=1, source_target_pairs={{0,14},{1,15},{2,0},{3,1},{4,2},{5,3},{6,4},{7,5},{8,6},{9,7},{10,... | collective-permute-start | bytes 589832 | tf_op jit(solution)/shard_map/ppermute | solution.py:30
  12.8 35.2 %collective-permute-start.4 = (bf16[384,512]{1,0:T(8,128)(2,1)S(1)}, bf16[384,512]{1,0:T(8,128)(2,1)S(1)}, u32[]{:S(2)}, u32[]{:S(2)}) collective-permute-start(bf16[384,512]{1,0:T(8,128)(2,1)S(1)} %get-tuple-element.18.both), channel_id=1, source_target_pairs={{0,16},{1,17},{2,18},{3,19},{4,20},{5,21},{6,22},{7,23},{8,24},{9,... | collective-permute-start | bytes 1179656 | tf_op jit(solution)/shard_map/ppermute | solution.py:24
  27.4 26.2 %collective-permute-start.5 = (bf16[384,512]{1,0:T(8,128)(2,1)S(1)}, bf16[384,512]{1,0:T(8,128)(2,1)S(1)}, u32[]{:S(2)}, u32[]{:S(2)}) collective-permute-start(bf16[384,512]{1,0:T(8,128)(2,1)S(1)} %collective-permute-done.refs_0_), channel_id=1, source_target_pairs={{0,2},{1,3},{2,4},{3,5},{4,6},{5,7},{6,8},{7,9},{8,10},{9,11},{10,... | collective-permute-start | bytes 1179656 | tf_op jit(solution)/shard_map/ppermute | solution.py:24
  29.3 17.7 %collective-permute-start.3 = (bf16[192,512]{1,0:T(8,128)(2,1)S(1)}, bf16[192,512]{1,0:T(8,128)(2,1)S(1)}, u32[]{:S(2)}, u32[]{:S(2)}) collective-permute-start(bf16[192,512]{1,0:T(8,128)(2,1)S(1)} %get-tuple-element.24), channel_id=1, source_target_pairs={{0,8},{1,9},{2,10},{3,11},{4,12},{5,13},{6,14},{7,15},{8,16},{9,17... | collective-permute-start | bytes 589832 | tf_op jit(solution)/shard_map/ppermute | solution.py:24
  31.2 29.8 %collective-permute-start.6 = (bf16[192,512]{1,0:T(8,128)(2,1)S(1)}, bf16[192,512]{1,0:T(8,128)(2,1)S(1)}, u32[]{:S(2)}, u32[]{:S(2)}) collective-permute-start(bf16[192,512]{1,0:T(8,128)(2,1)S(1)} %collective-permute-done.2), channel_id=1, source_target_pairs={{0,10},{1,11},{2,12},{3,13},{4,14},{5,15},{6,16},{7,17},{8,18},{9,... | collective-permute-start | bytes 589832 | tf_op jit(solution)/shard_map/ppermute | solution.py:30
  33.2 1.1 %copy-start.1 = (bf16[384,1024]{1,0:T(8,128)(2,1)S(1)}, bf16[384,1024]{1,0:T(8,128)(2,1)}, u32[]{:S(2)}) copy-start(bf16[384,1024]{1,0:T(8,128)(2,1)} %queries.7) | copy-start | bytes 2359300
  34.3 13.6 %copy-start.2 = (bf16[384,1024]{1,0:T(8,128)(2,1)S(1)}, bf16[384,1024]{1,0:T(8,128)(2,1)}, u32[]{:S(2)}) copy-start(bf16[384,1024]{1,0:T(8,128)(2,1)} %queries.7) | copy-start | bytes 2359300
  53.6 7.5 %copy-start = (bf16[1024,2048]{1,0:T(8,128)(2,1)S(1)}, bf16[1024,2048]{1,0:T(8,128)(2,1)}, u32[]{:S(2)}) copy-start(bf16[1024,2048]{1,0:T(8,128)(2,1)} %refs_1_.1) | copy-start | bytes 12582916

commit v3 on v2

--- a/solution.py
+++ b/solution.py
@@ -30,16 +30,15 @@
     return lax.ppermute(block, "seq", routes)
 
 
-def back(c, hops):
-    return c - hops if c % RING >= hops else c - hops + RING
-
-
-def from_back(c, hops):
-    return (c + hops if c % RING + hops < RING else c + hops - RING) + 4
-
-
-def pack_kernel(keys, values, both, tail, *rest):
-    *halves, sems = rest
+def stop_of(c, left):
+    return along(c + 4, left)
+
+
+def along(c, hops):
+    return c // RING * RING + (c + hops) % RING
+
+
+def pack_kernel(keys, values, both, tail, part, sems):
     rows, width = keys.shape
     copies = [
         pltpu.make_async_copy(source, both.at[:, pl.ds(n * width, width)], sems.at[n])
@@ -50,15 +49,13 @@
     for copy in copies:
         copy.wait()
     tail[...] = both[rows - tail.shape[0] :]
-    first = 0
-    for half in halves:
-        half[...] = both[first : first + half.shape[0]]
-        first += half.shape[0]
-
-
-def pack(keys, values, split=None):
+    part[...] = both[: part.shape[0]]
+
+
+def pack(keys, values, split):
     rows, width = keys.shape
-    counts = [rows, rows // 2] + ([split, rows - split] if split else [])
+    counts = [rows, rows // 2, split]
+    keys, values = (pltpu.with_memory_space_constraint(x, pltpu.HBM) for x in (keys, values))
     return pl.pallas_call(
         pack_kernel,
         out_shape=tuple(jax.ShapeDtypeStruct((n, 2 * width), keys.dtype) for n in counts),
@@ -145,7 +142,7 @@
 
 def add_parts(queries, pieces, acc_in, stats_in, acc, stats, flag):
     rows = queries.shape[0]
-    kv_width = pieces[0][0].shape[1] // 2
+    kv_width = pieces[0][0][0].shape[1] // 2
     kv_heads, group = sizes_of(queries, kv_width)
     tiles = tiles_of(rows, kv_heads)
     me = lax.axis_index("seq")
@@ -153,10 +150,13 @@
 
     def scores_with(parts, g, j):
         query = query_tile(queries, g, j, group)
-        return [scores_of(ref[:, g * HEAD : (g + 1) * HEAD], query) for ref, _ in parts]
-
-    def values_of(ref, g):
-        return ref[:, kv_width + g * HEAD : kv_width + (g + 1) * HEAD]
+        return [scores_of(columns_of(refs, g * HEAD), query) for refs, _ in parts]
+
+    def columns_of(refs, first):
+        return jnp.concatenate([ref[:, first : first + HEAD] for ref in refs], axis=0)
+
+    def values_of(refs, g):
+        return columns_of(refs, kv_width + g * HEAD)
 
     def same_top(parts):
         largest = []
@@ -221,17 +221,24 @@
         new_top()
 
 
+def blocks_of(refs, distances):
+    pieces = []
+    for distance in dict.fromkeys(distances):
+        pieces.append(([ref for ref, d in zip(refs, distances) if d == distance], distance))
+    return pieces
+
+
 def far_kernel(distances, queries, acc_in, stats_in, *refs):
-    pieces = list(zip(refs[: len(distances)], distances))
+    pieces = blocks_of(refs, distances)
     acc, stats, flag = refs[len(distances) :]
     add_parts(queries, pieces, acc_in, stats_in, acc, stats, flag)
 
 
 def last_kernel(distances, queries, acc_in, stats_in, *refs):
-    pieces = list(zip(refs[: len(distances)], distances))
+    pieces = blocks_of(refs, distances)
     weight, out_hbm, acc, stats, flag, attended, staged, sems = refs[len(distances) :]
     rows = queries.shape[0]
-    kv_heads, group = sizes_of(queries, pieces[0][0].shape[1] // 2)
+    kv_heads, group = sizes_of(queries, pieces[0][0][0].shape[1] // 2)
     cuts, _, cut = staged.shape
     add_parts(queries, pieces, acc_in, stats_in, acc, stats, flag)
     for t, (g, j) in enumerate(tiles_of(rows, kv_heads)):
@@ -322,19 +329,20 @@
 
 
 def on_device(queries, keys, values, out_weight):
-    both, tail, part, rest = pack(keys, values, 192)
+    split = 256
+    both, tail, part = pack(keys, values, split)
     behind = shifted(both, 2)
-    part = routed(part, lambda c: back(c, 1))
+    part = routed(part, lambda c: stop_of(c, 3))
     before = shifted(tail, 1)
-    eighth_rest = shifted(rest, 8)
     later = shifted(both, 16)
     behind, before, part = lax.optimization_barrier((behind, before, part))
     fourth = shifted(behind, 2)
-    eighth_first = routed(part, lambda c: from_back(c, 1))
+    eighth_first = routed(part, lambda c: along(c, -3))
+    eighth_rest = shifted(behind[split:], 6)
     state = near(queries, both, before)
-    state = far(queries, state, (eighth_rest, later), (8, 16))
-    state = far(queries, state, (behind, fourth), (2, 4))
-    return last(queries, state, (eighth_first,), (8,), out_weight)
+    state = far(queries, state, (behind, later), (2, 16))
+    state = far(queries, state, (fourth,), (4,))
+    return last(queries, state, (eighth_first, eighth_rest), (8, 8), out_weight)
 
 
 def solution(mesh):

time: 65.8 us -> 59.9 us (0.910)
  waiting for transfers between devices: 21.8 us -> 14.1 us
  starting transfers between devices: 20.8 us -> 24.6 us
  local copies, waits for them, and re-layouts: 2.99 us -> 1.15 us
    ppermute x5, waiting for transfers between devices: 21.8 us -> 14.1 us  [shifted(): lax.ppermute(block, 'seq', [(i, (i + distance) % devices) for i in range(...]
    ppermute x5, starting transfers between devices: 13.5 us -> 17.3 us  [shifted(): lax.ppermute(block, 'seq', [(i, (i + distance) % devices) for i in range(...]
    unnamed x10 -> x6, local copies, waits for them, and re-layouts: 2.99 us -> 1.14 us
    pallas_call x2, Pallas kernels: 13.1 us -> 11.9 us  [far(): pl.pallas_call(functools.partial(far_kernel, distances), out_shape=tuple(...]
    pallas_call x1, Pallas kernels: 0.09 us -> 1.07 us  [pack(): pl.pallas_call(pack_kernel, out_shape=tuple((jax.ShapeDtypeStruct((n, 2 *...]
  transfers between devices with their start and end apart: 7 -> 7, of which waited for: 3 -> 2; matrix products, arithmetic and copies ran while one was open for 0% -> 0% of each run, Pallas kernels for 24% -> 24%
where the time goes in v3:
time: 59.9 us; the launch traced here: 59.3 us
  starting transfers between devices  24.6 us (41%)
  Pallas kernels  19.1 us (32%)
  waiting for transfers between devices  14.1 us (24%)
  local copies, waits for them, and re-layouts  1.15 us (2%)
    ppermute x5, starting transfers between devices, shifted(): lax.ppermute(block, 'seq', [(i, (i + distance) % devices) for i in range(...  17.3 us
    ppermute x5, waiting for transfers between devices, shifted(): lax.ppermute(block, 'seq', [(i, (i + distance) % devices) for i in range(...  14.1 us
    pallas_call x2, Pallas kernels, far(): pl.pallas_call(functools.partial(far_kernel, distances), out_shape=tuple(...  11.9 us
    ppermute x2, starting transfers between devices, routed(): return lax.ppermute(block, 'seq', routes)  7.3 us
    pallas_call x1, Pallas kernels, last(): pl.pallas_call(functools.partial(last_kernel, distances), out_shape=jax.S...  3.99 us
    pallas_call x1, Pallas kernels, near(): pl.pallas_call(near_kernel, out_shape=(jax.ShapeDtypeStruct((kv_heads * s...  2.14 us
  transfers between devices with their start and end apart: 7, of which 2 were waited for; matrix products, arithmetic and copies ran while one was open for 0% of the time, Pallas kernels for 24%

profile of v3, /device:TPU:6, one launch (start us, length us, event | category | flops | bytes accessed | tf_op | source)
XLA Modules:
  0.0 59.3 jit_solution(4058368088166035323)
XLA Ops:
  0.0 1.1 %pack.1 = (bf16[384,512]{1,0:T(8,128)(2,1)S(1)}, bf16[192,512]{1,0:T(8,128)(2,1)S(1)}, bf16[256,512]{1,0:T(8,128)(2,1)S(1)}) custom-call(bf16[384,256]{1,0:T(8,128)(2,1)} %keys.1, bf16[384,256]{1,0:T(8,128)(2,1)} %values.1), custom_call_target="tpu_custom_call" | custom-call | tf_op jit(solution)/shard_map/pack/pallas_call | solution.py:59
  1.1 3.5 %collective-permute-start = (bf16[384,512]{1,0:T(8,128)(2,1)S(1)}, bf16[384,512]{1,0:T(8,128)(2,1)S(1)}, u32[]{:S(2)}, u32[]{:S(2)}) collective-permute-start(bf16[384,512]{1,0:T(8,128)(2,1)S(1)} %get-tuple-element.17.both), channel_id=1, source_target_pairs={{0,2},{1,3},{2,4},{3,5},{4,6},{5,7},{6,8},{7,9},{8,10},{9,11},{10,... | collective-permute-start | bytes 1179656 | tf_op jit(solution)/shard_map/ppermute | solution.py:24
  4.6 5.4 %collective-permute-start.2 = (bf16[256,512]{1,0:T(8,128)(2,1)S(1)}, bf16[256,512]{1,0:T(8,128)(2,1)S(1)}, u32[]{:S(2)}, u32[]{:S(2)}) collective-permute-start(bf16[256,512]{1,0:T(8,128)(2,1)S(1)} %get-tuple-element.19), channel_id=1, source_target_pairs={{0,14},{1,15},{2,0},{3,1},{4,2},{5,3},{6,4},{7,5},{8,22},{9,23},{1... | collective-permute-start | bytes 786440 | tf_op jit(solution)/shard_map/ppermute | solution.py:30
  10.0 1.9 %collective-permute-start.1 = (bf16[192,512]{1,0:T(8,128)(2,1)S(1)}, bf16[192,512]{1,0:T(8,128)(2,1)S(1)}, u32[]{:S(2)}, u32[]{:S(2)}) collective-permute-start(bf16[192,512]{1,0:T(8,128)(2,1)S(1)} %get-tuple-element.18), channel_id=1, source_target_pairs={{0,1},{1,2},{2,3},{3,4},{4,5},{5,6},{6,7},{7,8},{8,9},{9,10},{10,1... | collective-permute-start | bytes 589832 | tf_op jit(solution)/shard_map/ppermute | solution.py:24
  11.9 4.3 %collective-permute-start.3 = (bf16[384,512]{1,0:T(8,128)(2,1)S(1)}, bf16[384,512]{1,0:T(8,128)(2,1)S(1)}, u32[]{:S(2)}, u32[]{:S(2)}) collective-permute-start(bf16[384,512]{1,0:T(8,128)(2,1)S(1)} %get-tuple-element.17.both), channel_id=1, source_target_pairs={{0,16},{1,17},{2,18},{3,19},{4,20},{5,21},{6,22},{7,23},{8,24},{9,... | collective-permute-start | bytes 1179656 | tf_op jit(solution)/shard_map/ppermute | solution.py:24
  16.2 10.3 %collective-permute-done.1.tail = bf16[192,512]{1,0:T(8,128)(2,1)S(1)} collective-permute-done((bf16[192,512]{1,0:T(8,128)(2,1)S(1)}, bf16[192,512]{1,0:T(8,128)(2,1)S(1)}, u32[]{:S(2)}, u32[]{:S(2)}) %collective-permute-start.1) | collective-permute-done | bytes 196640 | tf_op jit(solution)/shard_map/ppermute | solution.py:24
  26.5 0.0 collective-permute-done.2
  26.5 0.0 collective-permute-done.refs_0_
  26.5 1.9 %collective-permute-start.4 = (bf16[384,512]{1,0:T(8,128)(2,1)S(1)}, bf16[384,512]{1,0:T(8,128)(2,1)S(1)}, u32[]{:S(2)}, u32[]{:S(2)}) collective-permute-start(bf16[384,512]{1,0:T(8,128)(2,1)S(1)} %collective-permute-done.refs_0_), channel_id=1, source_target_pairs={{0,2},{1,3},{2,4},{3,5},{4,6},{5,7},{6,8},{7,9},{8,10},{9,11},{10,... | collective-permute-start | bytes 1179656 | tf_op jit(solution)/shard_map/ppermute | solution.py:24
  28.4 1.9 %collective-permute-start.5 = (bf16[256,512]{1,0:T(8,128)(2,1)S(1)}, bf16[256,512]{1,0:T(8,128)(2,1)S(1)}, u32[]{:S(2)}, u32[]{:S(2)}) collective-permute-start(bf16[256,512]{1,0:T(8,128)(2,1)S(1)} %collective-permute-done.2), channel_id=1, source_target_pairs={{0,10},{1,11},{2,12},{3,13},{4,14},{5,15},{6,0},{7,1},{8,2},{9,3},... | collective-permute-start | bytes 786440 | tf_op jit(solution)/shard_map/ppermute | solution.py:30
  30.4 5.7 %collective-permute-start.6 = (bf16[128,512]{1,0:T(8,128)(2,1)S(1)}, bf16[128,512]{1,0:T(8,128)(2,1)S(1)}, u32[]{:S(2)}, u32[]{:S(2)}) collective-permute-start(bf16[128,512]{1,0:T(8,128)(2,1)S(1)} %slice.3), channel_id=1, source_target_pairs={{0,6},{1,7},{2,8},{3,9},{4,10},{5,11},{6,12},{7,13},{8,14},{9,15},... | collective-permute-start | bytes 393224 | tf_op jit(solution)/shard_map/ppermute | solution.py:24
  36.1 0.0 copy-start.1
  36.1 1.1 %copy-done.1 = bf16[384,1024]{1,0:T(8,128)(2,1)S(1)} copy-done((bf16[384,1024]{1,0:T(8,128)(2,1)S(1)}, bf16[384,1024]{1,0:T(8,128)(2,1)}, u32[]{:S(2)}) %copy-start.1) | copy-done | bytes 786456
  37.2 0.0 copy-start.2
  37.2 2.1 %near.1 = (f32[6,128,512]{2,1,0:T(8,128)S(1)}, f32[16,512]{1,0:T(8,128)S(1)}) custom-call(bf16[384,1024]{1,0:T(8,128)(2,1)S(1)} %copy-done.1, bf16[384,512]{1,0:T(8,128)(2,1)S(1)} %get-tuple-element.17.both, bf16[192,512]{1,0:T(8,128)(2,1)S(1)} %collective-permute-done.1.tail), custom_call_target="tpu_custom_call" | custom-call | flops 503316480 | bytes 3801088 | tf_op jit(solution)/shard_map/near/pallas_call | solution.py:277
  39.4 3.8 %collective-permute-done.3.refs_1_ = bf16[384,512]{1,0:T(8,128)(2,1)S(1)} collective-permute-done((bf16[384,512]{1,0:T(8,128)(2,1)S(1)}, bf16[384,512]{1,0:T(8,128)(2,1)S(1)}, u32[]{:S(2)}, u32[]{:S(2)}) %collective-permute-start.3) | collective-permute-done | bytes 393248 | tf_op jit(solution)/shard_map/ppermute | solution.py:24
  43.2 0.0 copy-done.2
  43.2 0.0 copy-start
  43.2 7.3 %far.2 = (f32[6,128,512]{2,1,0:T(8,128)S(1)}, f32[16,512]{1,0:T(8,128)S(1)}) custom-call(bf16[384,1024]{1,0:T(8,128)(2,1)S(1)} %copy-done.2, f32[6,128,512]{2,1,0:T(8,128)S(1)} %get-tuple-element.21.acc_in, f32[16,512]{1,0:T(8,128)S(1)} %get-tuple-element.22.stats_in, bf16[384,512]{1,0:T(8,128)(2,1)S(1)} %collective-permute-done.refs_0_, ...), custom_call_target="tpu_custom_call" | custom-call | flops 1207959552 | bytes 4718592 | tf_op jit(solution)/shard_map/far/pallas_call | solution.py:295
  50.5 0.0 collective-permute-done.4.refs_0_
  50.5 4.6 %far.3 = (f32[6,128,512]{2,1,0:T(8,128)S(1)}, f32[16,512]{1,0:T(8,128)S(1)}) custom-call(bf16[384,1024]{1,0:T(8,128)(2,1)S(1)} %copy-done.2, f32[6,128,512]{2,1,0:T(8,128)S(1)} %get-tuple-element.24.acc_in, f32[16,512]{1,0:T(8,128)S(1)} %get-tuple-element.25.stats_in, bf16[384,512]{1,0:T(8,128)(2,1)S(1)} %collective-permute-done.4.refs_0_), custom_call_target="tpu_custom_call" | custom-call | flops 603979776 | bytes 3932160 | tf_op jit(solution)/shard_map/far/pallas_call | solution.py:295
  55.1 0.0 collective-permute-done.6.refs_1_
  55.1 0.0 collective-permute-done.5.refs_0_
  55.1 0.0 copy-done
  55.1 4.0 %last.1 = bf16[384,2048]{1,0:T(8,128)(2,1)} custom-call(bf16[384,1024]{1,0:T(8,128)(2,1)S(1)} %copy-done.2, f32[6,128,512]{2,1,0:T(8,128)S(1)} %get-tuple-element.26.acc_in, f32[16,512]{1,0:T(8,128)S(1)} %get-tuple-element.27.stats_in, bf16[256,512]{1,0:T(8,128)(2,1)S(1)} %collective-permute-done.5.refs_0_, ...), custom_call_target="tpu_custom_call" | custom-call | flops 2214592512 | bytes 3932160 | tf_op jit(solution)/shard_map/last/pallas_call | solution.py:312
  (1 shorter events, 0.0 us)
Async XLA Ops:
  1.1 25.4 %collective-permute-start = (bf16[384,512]{1,0:T(8,128)(2,1)S(1)}, bf16[384,512]{1,0:T(8,128)(2,1)S(1)}, u32[]{:S(2)}, u32[]{:S(2)}) collective-permute-start(bf16[384,512]{1,0:T(8,128)(2,1)S(1)} %get-tuple-element.17.both), channel_id=1, source_target_pairs={{0,2},{1,3},{2,4},{3,5},{4,6},{5,7},{6,8},{7,9},{8,10},{9,11},{10,... | collective-permute-start | bytes 1179656 | tf_op jit(solution)/shard_map/ppermute | solution.py:24
  4.6 21.9 %collective-permute-start.2 = (bf16[256,512]{1,0:T(8,128)(2,1)S(1)}, bf16[256,512]{1,0:T(8,128)(2,1)S(1)}, u32[]{:S(2)}, u32[]{:S(2)}) collective-permute-start(bf16[256,512]{1,0:T(8,128)(2,1)S(1)} %get-tuple-element.19), channel_id=1, source_target_pairs={{0,14},{1,15},{2,0},{3,1},{4,2},{5,3},{6,4},{7,5},{8,22},{9,23},{1... | collective-permute-start | bytes 786440 | tf_op jit(solution)/shard_map/ppermute | solution.py:30
  10.0 16.6 %collective-permute-start.1 = (bf16[192,512]{1,0:T(8,128)(2,1)S(1)}, bf16[192,512]{1,0:T(8,128)(2,1)S(1)}, u32[]{:S(2)}, u32[]{:S(2)}) collective-permute-start(bf16[192,512]{1,0:T(8,128)(2,1)S(1)} %get-tuple-element.18), channel_id=1, source_target_pairs={{0,1},{1,2},{2,3},{3,4},{4,5},{5,6},{6,7},{7,8},{8,9},{9,10},{10,1... | collective-permute-start | bytes 589832 | tf_op jit(solution)/shard_map/ppermute | solution.py:24
  11.9 31.3 %collective-permute-start.3 = (bf16[384,512]{1,0:T(8,128)(2,1)S(1)}, bf16[384,512]{1,0:T(8,128)(2,1)S(1)}, u32[]{:S(2)}, u32[]{:S(2)}) collective-permute-start(bf16[384,512]{1,0:T(8,128)(2,1)S(1)} %get-tuple-element.17.both), channel_id=1, source_target_pairs={{0,16},{1,17},{2,18},{3,19},{4,20},{5,21},{6,22},{7,23},{8,24},{9,... | collective-permute-start | bytes 1179656 | tf_op jit(solution)/shard_map/ppermute | solution.py:24
  26.5 23.9 %collective-permute-start.4 = (bf16[384,512]{1,0:T(8,128)(2,1)S(1)}, bf16[384,512]{1,0:T(8,128)(2,1)S(1)}, u32[]{:S(2)}, u32[]{:S(2)}) collective-permute-start(bf16[384,512]{1,0:T(8,128)(2,1)S(1)} %collective-permute-done.refs_0_), channel_id=1, source_target_pairs={{0,2},{1,3},{2,4},{3,5},{4,6},{5,7},{6,8},{7,9},{8,10},{9,11},{10,... | collective-permute-start | bytes 1179656 | tf_op jit(solution)/shard_map/ppermute | solution.py:24
  28.4 26.7 %collective-permute-start.5 = (bf16[256,512]{1,0:T(8,128)(2,1)S(1)}, bf16[256,512]{1,0:T(8,128)(2,1)S(1)}, u32[]{:S(2)}, u32[]{:S(2)}) collective-permute-start(bf16[256,512]{1,0:T(8,128)(2,1)S(1)} %collective-permute-done.2), channel_id=1, source_target_pairs={{0,10},{1,11},{2,12},{3,13},{4,14},{5,15},{6,0},{7,1},{8,2},{9,3},... | collective-permute-start | bytes 786440 | tf_op jit(solution)/shard_map/ppermute | solution.py:30
  30.4 24.7 %collective-permute-start.6 = (bf16[128,512]{1,0:T(8,128)(2,1)S(1)}, bf16[128,512]{1,0:T(8,128)(2,1)S(1)}, u32[]{:S(2)}, u32[]{:S(2)}) collective-permute-start(bf16[128,512]{1,0:T(8,128)(2,1)S(1)} %slice.3), channel_id=1, source_target_pairs={{0,6},{1,7},{2,8},{3,9},{4,10},{5,11},{6,12},{7,13},{8,14},{9,15},... | collective-permute-start | bytes 393224 | tf_op jit(solution)/shard_map/ppermute | solution.py:24
  36.1 1.1 %copy-start.1 = (bf16[384,1024]{1,0:T(8,128)(2,1)S(1)}, bf16[384,1024]{1,0:T(8,128)(2,1)}, u32[]{:S(2)}) copy-start(bf16[384,1024]{1,0:T(8,128)(2,1)} %queries.7) | copy-start | bytes 2359300
  37.2 5.9 %copy-start.2 = (bf16[384,1024]{1,0:T(8,128)(2,1)S(1)}, bf16[384,1024]{1,0:T(8,128)(2,1)}, u32[]{:S(2)}) copy-start(bf16[384,1024]{1,0:T(8,128)(2,1)} %queries.7) | copy-start | bytes 2359300
  43.2 11.9 %copy-start = (bf16[1024,2048]{1,0:T(8,128)(2,1)S(1)}, bf16[1024,2048]{1,0:T(8,128)(2,1)}, u32[]{:S(2)}) copy-start(bf16[1024,2048]{1,0:T(8,128)(2,1)} %refs_2_.1) | copy-start | bytes 12582916

commit v4 on v3

--- a/solution.py
+++ b/solution.py
@@ -307,7 +307,7 @@
 def last(queries, state, blocks, distances, out_weight):
     rows, width = queries.shape
     wide = out_weight.shape[1]
-    cut = 512
+    cut = 256
     acc, stats = state
     return pl.pallas_call(
         functools.partial(last_kernel, distances),

time: 59.9 us -> 59.9 us (level)
  no operation moved by 1% of the time
where the time goes in v4:
time: 59.9 us; the launch traced here: 59.4 us
  starting transfers between devices  24.6 us (41%)
  Pallas kernels  19.2 us (32%)
  waiting for transfers between devices  14.1 us (24%)
  local copies, waits for them, and re-layouts  1.15 us (2%)
    ppermute x5, starting transfers between devices, shifted(): lax.ppermute(block, 'seq', [(i, (i + distance) % devices) for i in range(...  17.3 us
    ppermute x5, waiting for transfers between devices, shifted(): lax.ppermute(block, 'seq', [(i, (i + distance) % devices) for i in range(...  14.1 us
    pallas_call x2, Pallas kernels, far(): pl.pallas_call(functools.partial(far_kernel, distances), out_shape=tuple(...  11.9 us
    ppermute x2, starting transfers between devices, routed(): return lax.ppermute(block, 'seq', routes)  7.3 us
    pallas_call x1, Pallas kernels, last(): pl.pallas_call(functools.partial(last_kernel, distances), out_shape=jax.S...  4.07 us
    pallas_call x1, Pallas kernels, near(): pl.pallas_call(near_kernel, out_shape=(jax.ShapeDtypeStruct((kv_heads * s...  2.14 us
  transfers between devices with their start and end apart: 7, of which 2 were waited for; matrix products, arithmetic and copies ran while one was open for 0% of the time, Pallas kernels for 24%

profile of v4, /device:TPU:6, one launch (start us, length us, event | category | flops | bytes accessed | tf_op | source)
XLA Modules:
  0.0 59.4 jit_solution(1213370530508563375)
XLA Ops:
  0.0 1.1 %pack.1 = (bf16[384,512]{1,0:T(8,128)(2,1)S(1)}, bf16[192,512]{1,0:T(8,128)(2,1)S(1)}, bf16[256,512]{1,0:T(8,128)(2,1)S(1)}) custom-call(bf16[384,256]{1,0:T(8,128)(2,1)} %keys.1, bf16[384,256]{1,0:T(8,128)(2,1)} %values.1), custom_call_target="tpu_custom_call" | custom-call | tf_op jit(solution)/shard_map/pack/pallas_call | solution.py:59
  1.1 3.5 %collective-permute-start = (bf16[384,512]{1,0:T(8,128)(2,1)S(1)}, bf16[384,512]{1,0:T(8,128)(2,1)S(1)}, u32[]{:S(2)}, u32[]{:S(2)}) collective-permute-start(bf16[384,512]{1,0:T(8,128)(2,1)S(1)} %get-tuple-element.17.both), channel_id=1, source_target_pairs={{0,2},{1,3},{2,4},{3,5},{4,6},{5,7},{6,8},{7,9},{8,10},{9,11},{10,... | collective-permute-start | bytes 1179656 | tf_op jit(solution)/shard_map/ppermute | solution.py:24
  4.6 5.4 %collective-permute-start.2 = (bf16[256,512]{1,0:T(8,128)(2,1)S(1)}, bf16[256,512]{1,0:T(8,128)(2,1)S(1)}, u32[]{:S(2)}, u32[]{:S(2)}) collective-permute-start(bf16[256,512]{1,0:T(8,128)(2,1)S(1)} %get-tuple-element.19), channel_id=1, source_target_pairs={{0,14},{1,15},{2,0},{3,1},{4,2},{5,3},{6,4},{7,5},{8,22},{9,23},{1... | collective-permute-start | bytes 786440 | tf_op jit(solution)/shard_map/ppermute | solution.py:30
  10.0 1.9 %collective-permute-start.1 = (bf16[192,512]{1,0:T(8,128)(2,1)S(1)}, bf16[192,512]{1,0:T(8,128)(2,1)S(1)}, u32[]{:S(2)}, u32[]{:S(2)}) collective-permute-start(bf16[192,512]{1,0:T(8,128)(2,1)S(1)} %get-tuple-element.18), channel_id=1, source_target_pairs={{0,1},{1,2},{2,3},{3,4},{4,5},{5,6},{6,7},{7,8},{8,9},{9,10},{10,1... | collective-permute-start | bytes 589832 | tf_op jit(solution)/shard_map/ppermute | solution.py:24
  11.9 4.3 %collective-permute-start.3 = (bf16[384,512]{1,0:T(8,128)(2,1)S(1)}, bf16[384,512]{1,0:T(8,128)(2,1)S(1)}, u32[]{:S(2)}, u32[]{:S(2)}) collective-permute-start(bf16[384,512]{1,0:T(8,128)(2,1)S(1)} %get-tuple-element.17.both), channel_id=1, source_target_pairs={{0,16},{1,17},{2,18},{3,19},{4,20},{5,21},{6,22},{7,23},{8,24},{9,... | collective-permute-start | bytes 1179656 | tf_op jit(solution)/shard_map/ppermute | solution.py:24
  16.2 10.3 %collective-permute-done.1.tail = bf16[192,512]{1,0:T(8,128)(2,1)S(1)} collective-permute-done((bf16[192,512]{1,0:T(8,128)(2,1)S(1)}, bf16[192,512]{1,0:T(8,128)(2,1)S(1)}, u32[]{:S(2)}, u32[]{:S(2)}) %collective-permute-start.1) | collective-permute-done | bytes 196640 | tf_op jit(solution)/shard_map/ppermute | solution.py:24
  26.5 0.0 collective-permute-done.2
  26.5 0.0 collective-permute-done.refs_0_
  26.5 1.9 %collective-permute-start.4 = (bf16[384,512]{1,0:T(8,128)(2,1)S(1)}, bf16[384,512]{1,0:T(8,128)(2,1)S(1)}, u32[]{:S(2)}, u32[]{:S(2)}) collective-permute-start(bf16[384,512]{1,0:T(8,128)(2,1)S(1)} %collective-permute-done.refs_0_), channel_id=1, source_target_pairs={{0,2},{1,3},{2,4},{3,5},{4,6},{5,7},{6,8},{7,9},{8,10},{9,11},{10,... | collective-permute-start | bytes 1179656 | tf_op jit(solution)/shard_map/ppermute | solution.py:24
  28.4 1.9 %collective-permute-start.5 = (bf16[256,512]{1,0:T(8,128)(2,1)S(1)}, bf16[256,512]{1,0:T(8,128)(2,1)S(1)}, u32[]{:S(2)}, u32[]{:S(2)}) collective-permute-start(bf16[256,512]{1,0:T(8,128)(2,1)S(1)} %collective-permute-done.2), channel_id=1, source_target_pairs={{0,10},{1,11},{2,12},{3,13},{4,14},{5,15},{6,0},{7,1},{8,2},{9,3},... | collective-permute-start | bytes 786440 | tf_op jit(solution)/shard_map/ppermute | solution.py:30
  30.4 5.7 %collective-permute-start.6 = (bf16[128,512]{1,0:T(8,128)(2,1)S(1)}, bf16[128,512]{1,0:T(8,128)(2,1)S(1)}, u32[]{:S(2)}, u32[]{:S(2)}) collective-permute-start(bf16[128,512]{1,0:T(8,128)(2,1)S(1)} %slice.3), channel_id=1, source_target_pairs={{0,6},{1,7},{2,8},{3,9},{4,10},{5,11},{6,12},{7,13},{8,14},{9,15},... | collective-permute-start | bytes 393224 | tf_op jit(solution)/shard_map/ppermute | solution.py:24
  36.1 0.0 copy-start.1
  36.1 1.1 %copy-done.1 = bf16[384,1024]{1,0:T(8,128)(2,1)S(1)} copy-done((bf16[384,1024]{1,0:T(8,128)(2,1)S(1)}, bf16[384,1024]{1,0:T(8,128)(2,1)}, u32[]{:S(2)}) %copy-start.1) | copy-done | bytes 786456
  37.2 0.0 copy-start.2
  37.2 2.1 %near.1 = (f32[6,128,512]{2,1,0:T(8,128)S(1)}, f32[16,512]{1,0:T(8,128)S(1)}) custom-call(bf16[384,1024]{1,0:T(8,128)(2,1)S(1)} %copy-done.1, bf16[384,512]{1,0:T(8,128)(2,1)S(1)} %get-tuple-element.17.both, bf16[192,512]{1,0:T(8,128)(2,1)S(1)} %collective-permute-done.1.tail), custom_call_target="tpu_custom_call" | custom-call | flops 503316480 | bytes 3801088 | tf_op jit(solution)/shard_map/near/pallas_call | solution.py:277
  39.4 3.8 %collective-permute-done.3.refs_1_ = bf16[384,512]{1,0:T(8,128)(2,1)S(1)} collective-permute-done((bf16[384,512]{1,0:T(8,128)(2,1)S(1)}, bf16[384,512]{1,0:T(8,128)(2,1)S(1)}, u32[]{:S(2)}, u32[]{:S(2)}) %collective-permute-start.3) | collective-permute-done | bytes 393248 | tf_op jit(solution)/shard_map/ppermute | solution.py:24
  43.2 0.0 copy-done.2
  43.2 0.0 copy-start
  43.2 7.3 %far.2 = (f32[6,128,512]{2,1,0:T(8,128)S(1)}, f32[16,512]{1,0:T(8,128)S(1)}) custom-call(bf16[384,1024]{1,0:T(8,128)(2,1)S(1)} %copy-done.2, f32[6,128,512]{2,1,0:T(8,128)S(1)} %get-tuple-element.21.acc_in, f32[16,512]{1,0:T(8,128)S(1)} %get-tuple-element.22.stats_in, bf16[384,512]{1,0:T(8,128)(2,1)S(1)} %collective-permute-done.refs_0_, ...), custom_call_target="tpu_custom_call" | custom-call | flops 1207959552 | bytes 4718592 | tf_op jit(solution)/shard_map/far/pallas_call | solution.py:295
  50.5 0.0 collective-permute-done.4.refs_0_
  50.5 4.6 %far.3 = (f32[6,128,512]{2,1,0:T(8,128)S(1)}, f32[16,512]{1,0:T(8,128)S(1)}) custom-call(bf16[384,1024]{1,0:T(8,128)(2,1)S(1)} %copy-done.2, f32[6,128,512]{2,1,0:T(8,128)S(1)} %get-tuple-element.24.acc_in, f32[16,512]{1,0:T(8,128)S(1)} %get-tuple-element.25.stats_in, bf16[384,512]{1,0:T(8,128)(2,1)S(1)} %collective-permute-done.4.refs_0_), custom_call_target="tpu_custom_call" | custom-call | flops 603979776 | bytes 3932160 | tf_op jit(solution)/shard_map/far/pallas_call | solution.py:295
  55.1 0.0 collective-permute-done.6.refs_1_
  55.1 0.0 collective-permute-done.5.refs_0_
  55.1 0.0 copy-done
  55.1 4.1 %last.1 = bf16[384,2048]{1,0:T(8,128)(2,1)} custom-call(bf16[384,1024]{1,0:T(8,128)(2,1)S(1)} %copy-done.2, f32[6,128,512]{2,1,0:T(8,128)S(1)} %get-tuple-element.26.acc_in, f32[16,512]{1,0:T(8,128)S(1)} %get-tuple-element.27.stats_in, bf16[256,512]{1,0:T(8,128)(2,1)S(1)} %collective-permute-done.5.refs_0_, ...), custom_call_target="tpu_custom_call" | custom-call | flops 2214592512 | bytes 3932160 | tf_op jit(solution)/shard_map/last/pallas_call | solution.py:312
  (1 shorter events, 0.0 us)
Async XLA Ops:
  1.1 25.4 %collective-permute-start = (bf16[384,512]{1,0:T(8,128)(2,1)S(1)}, bf16[384,512]{1,0:T(8,128)(2,1)S(1)}, u32[]{:S(2)}, u32[]{:S(2)}) collective-permute-start(bf16[384,512]{1,0:T(8,128)(2,1)S(1)} %get-tuple-element.17.both), channel_id=1, source_target_pairs={{0,2},{1,3},{2,4},{3,5},{4,6},{5,7},{6,8},{7,9},{8,10},{9,11},{10,... | collective-permute-start | bytes 1179656 | tf_op jit(solution)/shard_map/ppermute | solution.py:24
  4.6 21.9 %collective-permute-start.2 = (bf16[256,512]{1,0:T(8,128)(2,1)S(1)}, bf16[256,512]{1,0:T(8,128)(2,1)S(1)}, u32[]{:S(2)}, u32[]{:S(2)}) collective-permute-start(bf16[256,512]{1,0:T(8,128)(2,1)S(1)} %get-tuple-element.19), channel_id=1, source_target_pairs={{0,14},{1,15},{2,0},{3,1},{4,2},{5,3},{6,4},{7,5},{8,22},{9,23},{1... | collective-permute-start | bytes 786440 | tf_op jit(solution)/shard_map/ppermute | solution.py:30
  10.0 16.6 %collective-permute-start.1 = (bf16[192,512]{1,0:T(8,128)(2,1)S(1)}, bf16[192,512]{1,0:T(8,128)(2,1)S(1)}, u32[]{:S(2)}, u32[]{:S(2)}) collective-permute-start(bf16[192,512]{1,0:T(8,128)(2,1)S(1)} %get-tuple-element.18), channel_id=1, source_target_pairs={{0,1},{1,2},{2,3},{3,4},{4,5},{5,6},{6,7},{7,8},{8,9},{9,10},{10,1... | collective-permute-start | bytes 589832 | tf_op jit(solution)/shard_map/ppermute | solution.py:24
  11.9 31.3 %collective-permute-start.3 = (bf16[384,512]{1,0:T(8,128)(2,1)S(1)}, bf16[384,512]{1,0:T(8,128)(2,1)S(1)}, u32[]{:S(2)}, u32[]{:S(2)}) collective-permute-start(bf16[384,512]{1,0:T(8,128)(2,1)S(1)} %get-tuple-element.17.both), channel_id=1, source_target_pairs={{0,16},{1,17},{2,18},{3,19},{4,20},{5,21},{6,22},{7,23},{8,24},{9,... | collective-permute-start | bytes 1179656 | tf_op jit(solution)/shard_map/ppermute | solution.py:24
  26.5 23.9 %collective-permute-start.4 = (bf16[384,512]{1,0:T(8,128)(2,1)S(1)}, bf16[384,512]{1,0:T(8,128)(2,1)S(1)}, u32[]{:S(2)}, u32[]{:S(2)}) collective-permute-start(bf16[384,512]{1,0:T(8,128)(2,1)S(1)} %collective-permute-done.refs_0_), channel_id=1, source_target_pairs={{0,2},{1,3},{2,4},{3,5},{4,6},{5,7},{6,8},{7,9},{8,10},{9,11},{10,... | collective-permute-start | bytes 1179656 | tf_op jit(solution)/shard_map/ppermute | solution.py:24
  28.4 26.7 %collective-permute-start.5 = (bf16[256,512]{1,0:T(8,128)(2,1)S(1)}, bf16[256,512]{1,0:T(8,128)(2,1)S(1)}, u32[]{:S(2)}, u32[]{:S(2)}) collective-permute-start(bf16[256,512]{1,0:T(8,128)(2,1)S(1)} %collective-permute-done.2), channel_id=1, source_target_pairs={{0,10},{1,11},{2,12},{3,13},{4,14},{5,15},{6,0},{7,1},{8,2},{9,3},... | collective-permute-start | bytes 786440 | tf_op jit(solution)/shard_map/ppermute | solution.py:30
  30.4 24.7 %collective-permute-start.6 = (bf16[128,512]{1,0:T(8,128)(2,1)S(1)}, bf16[128,512]{1,0:T(8,128)(2,1)S(1)}, u32[]{:S(2)}, u32[]{:S(2)}) collective-permute-start(bf16[128,512]{1,0:T(8,128)(2,1)S(1)} %slice.3), channel_id=1, source_target_pairs={{0,6},{1,7},{2,8},{3,9},{4,10},{5,11},{6,12},{7,13},{8,14},{9,15},... | collective-permute-start | bytes 393224 | tf_op jit(solution)/shard_map/ppermute | solution.py:24
  36.1 1.1 %copy-start.1 = (bf16[384,1024]{1,0:T(8,128)(2,1)S(1)}, bf16[384,1024]{1,0:T(8,128)(2,1)}, u32[]{:S(2)}) copy-start(bf16[384,1024]{1,0:T(8,128)(2,1)} %queries.7) | copy-start | bytes 2359300
  37.2 5.9 %copy-start.2 = (bf16[384,1024]{1,0:T(8,128)(2,1)S(1)}, bf16[384,1024]{1,0:T(8,128)(2,1)}, u32[]{:S(2)}) copy-start(bf16[384,1024]{1,0:T(8,128)(2,1)} %queries.7) | copy-start | bytes 2359300
  43.2 11.9 %copy-start = (bf16[1024,2048]{1,0:T(8,128)(2,1)S(1)}, bf16[1024,2048]{1,0:T(8,128)(2,1)}, u32[]{:S(2)}) copy-start(bf16[1024,2048]{1,0:T(8,128)(2,1)} %refs_2_.1) | copy-start | bytes 12582916
